TPU v7x, 32 devices: a whole 2x2x4 slice. The times are simulated.
32 devices in a mesh: dp: 16 (over z, y, x), fsdp: 2 (over core).
Axes of the slice: x: 2, y: 2, z: 4, core: 2. Of those that a mesh axis runs over, the one named last changes fastest.
Arguments:
- tokens: bfloat16 [8192, 1536], P(('dp', 'fsdp')), may hold values from -6 to 6
- cotangent: bfloat16 [8192, 1536], P(('dp', 'fsdp')), may hold values from -6 to 6
- deal: int32 [8192], P(('dp', 'fsdp')), may hold values from 0 to 8191, as said below
- first_len: int32 [2], replicated, may hold values from 1365 to 4096, as said below
- w_query: bfloat16 [1536, 1536], P('dp', 'fsdp'), may hold values from -0.15625 to 0.15625
- w_key: bfloat16 [1536, 128], P('dp', 'fsdp'), may hold values from -0.15625 to 0.15625
- w_value: bfloat16 [1536, 128], P('dp', 'fsdp'), may hold values from -0.15625 to 0.15625
- w_out: bfloat16 [1536, 1536], P('fsdp', 'dp'), may hold values from -3 to 3
- w_gate: bfloat16 [1536, 4608], P('dp', 'fsdp'), may hold values from -0.15625 to 0.15625
- w_up: bfloat16 [1536, 4608], P('dp', 'fsdp'), may hold values from -0.15625 to 0.15625
- w_down: bfloat16 [4608, 1536], P('fsdp', 'dp'), may hold values from -0.09375 to 0.09375
- norm_gains: bfloat16 [2, 1536], P('fsdp', 'dp'), may hold values from 0.25 to 1.75
Outputs:
- output: bfloat16 [8192, 1536], P(('dp', 'fsdp'))
- input_grad: bfloat16 [8192, 1536], P(('dp', 'fsdp'))
- grad_query: float32 [1536, 1536], P('dp', 'fsdp')
- grad_key: float32 [1536, 128], P('dp', 'fsdp')
- grad_value: float32 [1536, 128], P('dp', 'fsdp')
- grad_out: float32 [1536, 1536], P('fsdp', 'dp')
- grad_gate: float32 [1536, 4608], P('dp', 'fsdp')
- grad_up: float32 [1536, 4608], P('dp', 'fsdp')
- grad_down: float32 [4608, 1536], P('fsdp', 'dp')
- grad_gains: float32 [2, 1536], P('fsdp', 'dp')
Inputs may be any that keep to these rules, and one draw needn't show every extreme that they name: deal is a permutation of 0 to 8191. The 256 packed positions of block b = d * 2 + f (blocks of 256 along the array) name exactly 16 rows of each block e * 2 + f, e < 16, and no other rows. In one stream, drawn from the seed, first_len is 4096: that stream holds a single sequence. In every other stream first_len is at most 2731, and its second sequence has 4096 - first_len rows.
All inputs are finite; a program needn't handle non-finite values.
Results may differ from a plain program's by a relative error of at most 0.017.
Values may be sent and summed in bfloat16 or wider, within the bound.
A program may use at most 320 MiB of HBM per device.

v0:
```python
import jax
import jax.numpy as jnp
from jax import lax
from jax.sharding import PartitionSpec as P

HEADS = 12
HEAD = 128
WINDOW = 1024
MICRO = 2


EPSILON = 1e-06
NEGATIVE = -1e30


def passed_along(x, axis, by):
    count = lax.axis_size(axis)
    pairs = [(i, i + by) for i in range(count) if 0 <= i + by < count]
    return lax.ppermute(x, axis, pairs)


def normed(row_values, gain_row):
    return (
        row_values
        * lax.rsqrt(jnp.mean(row_values * row_values, axis=-1, keepdims=True) + EPSILON)
        * gain_row
    )


def rotate(values, cosine, sine_table):
    half_width = values.shape[-1] // 2
    front_half = values[..., :half_width]
    back_half = values[..., half_width:]
    return jnp.concatenate(
        [
            front_half * cosine - back_half * sine_table,
            back_half * cosine + front_half * sine_table,
        ],
        axis=-1,
    )


def angles(places):
    half_width = HEAD // 2
    frequency = 10000.0 ** (-jnp.arange(half_width, dtype=jnp.float32) * 2.0 / HEAD)
    angle_rows = places.astype(jnp.float32)[:, None] * frequency[None, :]
    return (jnp.cos(angle_rows), jnp.sin(angle_rows))


def contract_rows(left, right):
    return lax.dot_general(
        left, right, (((0,), (0,)), ((), ())), preferred_element_type=jnp.float32
    )


def against(left, right):
    return lax.dot_general(
        left, right, (((1,), (1,)), ((), ())), preferred_element_type=jnp.float32
    )


def gelu_tanh(inputs):
    return jax.nn.gelu(inputs, approximate=True)


def per_device(
    tokens,
    cotangent,
    deal,
    first_len,
    w_query,
    w_key,
    w_value,
    w_out,
    w_gate,
    w_up,
    w_down,
    norm_gains,
):
    peer_count = lax.axis_size("dp")
    core_count = lax.axis_size("fsdp")
    device_total = peer_count * core_count
    row_count = tokens.shape[0]
    model_width = tokens.shape[1]
    per_peer = row_count // peer_count
    micro_rows = row_count // MICRO
    reach_steps = min(device_total - 1, (WINDOW + micro_rows - 2) // micro_rows)
    linear = lax.axis_index("dp") * core_count + lax.axis_index("fsdp")
    source_peer = deal // (row_count * core_count)
    offsets = deal % row_count
    bucket_order = jnp.argsort(source_peer, stable=True)
    inverse = jnp.argsort(bucket_order)
    wanted = offsets[bucket_order].reshape(peer_count, per_peer)
    requested = lax.all_to_all(wanted, "dp", split_axis=0, concat_axis=0, tiled=True)
    picked = requested.reshape(-1)
    fetched = (
        lax.all_to_all(
            tokens[picked].reshape(peer_count, per_peer, model_width),
            "dp",
            split_axis=0,
            concat_axis=0,
            tiled=True,
        ),
        lax.all_to_all(
            cotangent[picked].reshape(peer_count, per_peer, model_width),
            "dp",
            split_axis=0,
            concat_axis=0,
            tiled=True,
        ),
    )
    rows_in = fetched[0].reshape(row_count, model_width)[inverse]
    grad_in = fetched[1].reshape(row_count, model_width)[inverse]
    halves = (
        lax.all_gather(w_query, "dp", axis=0, tiled=True),
        lax.all_gather(w_key, "dp", axis=0, tiled=True),
        lax.all_gather(w_value, "dp", axis=0, tiled=True),
        lax.all_gather(w_out, "dp", axis=1, tiled=True),
        lax.all_gather(w_gate, "dp", axis=0, tiled=True),
        lax.all_gather(w_up, "dp", axis=0, tiled=True),
        lax.all_gather(w_down, "dp", axis=1, tiled=True),
        lax.all_gather(norm_gains, "dp", axis=1, tiled=True),
    )
    gathered = (
        lax.all_gather(halves[0], "fsdp", axis=1, tiled=True),
        lax.all_gather(halves[1], "fsdp", axis=1, tiled=True),
        lax.all_gather(halves[2], "fsdp", axis=1, tiled=True),
        lax.all_gather(halves[3], "fsdp", axis=0, tiled=True),
        lax.all_gather(halves[4], "fsdp", axis=1, tiled=True),
        lax.all_gather(halves[5], "fsdp", axis=1, tiled=True),
        lax.all_gather(halves[6], "fsdp", axis=0, tiled=True),
        lax.all_gather(halves[7], "fsdp", axis=0, tiled=True),
    )
    full_query, full_key, full_value, full_out, full_gate, full_up, full_down, full_gains = gathered
    gain_one = full_gains[0].astype(jnp.float32)
    gain_two = full_gains[1].astype(jnp.float32)
    inside = jnp.arange(micro_rows, dtype=jnp.int32)
    query_place = linear * micro_rows + inside
    query_later = query_place[None, :] >= first_len[:, None]
    query_within = query_place[None, :] - jnp.where(query_later, first_len[:, None], 0)
    distance = jnp.arange(reach_steps, -1, -1, dtype=jnp.int32)
    key_place = ((linear - distance)[:, None] * micro_rows + inside[None, :]).reshape(-1)
    key_later = key_place[None, :] >= first_len[:, None]
    allowed = (
        (query_later[:, :, None] == key_later[:, None, :])
        & (key_place[None, None, :] >= 0)
        & (key_place[None, None, :] <= query_place[None, :, None])
        & (query_place[None, :, None] - key_place[None, None, :] < WINDOW)
    )
    rows_float = rows_in.astype(jnp.float32)
    cosine, sine_table = angles(query_within.reshape(-1))
    score_scale = HEAD ** (-0.5)
    normal_one = normed(rows_float, gain_one).astype(jnp.bfloat16)
    query_raw = jnp.dot(normal_one, full_query, preferred_element_type=jnp.float32).reshape(
        row_count, HEADS, HEAD
    )
    query_rows = rotate(query_raw, cosine[:, None, :], sine_table[:, None, :]).astype(jnp.bfloat16)
    key_rows = rotate(
        jnp.dot(normal_one, full_key, preferred_element_type=jnp.float32), cosine, sine_table
    ).astype(jnp.bfloat16)
    value_rows = jnp.dot(normal_one, full_value, preferred_element_type=jnp.float32).astype(
        jnp.bfloat16
    )
    earlier = []
    for distance_step in range(1, reach_steps + 1):
        earlier.append(passed_along((key_rows, value_rows), ("dp", "fsdp"), distance_step))
    ordered = earlier[::-1] + [(key_rows, value_rows)]
    all_keys = jnp.concatenate(
        [member[0].reshape(MICRO, micro_rows, HEAD) for member in ordered], axis=1
    )
    all_values = jnp.concatenate(
        [member[1].reshape(MICRO, micro_rows, HEAD) for member in ordered], axis=1
    )
    by_head = jnp.transpose(query_rows.reshape(MICRO, micro_rows, HEADS, HEAD), (2, 0, 1, 3))

    def attend(query_head):
        scores = jnp.where(
            allowed,
            jnp.einsum("mqd,mkd->mqk", query_head, all_keys, preferred_element_type=jnp.float32)
            * score_scale,
            NEGATIVE,
        )
        row_top = jnp.max(scores, axis=2, keepdims=True)
        exp_scores = jnp.exp(scores - row_top)
        row_total = jnp.sum(exp_scores, axis=2, keepdims=True)
        soft_weights = (exp_scores / row_total).astype(jnp.bfloat16)
        attended_head = jnp.einsum(
            "mqk,mkd->mqd", soft_weights, all_values, preferred_element_type=jnp.float32
        )
        return (attended_head, row_top[..., 0] + jnp.log(row_total[..., 0]))

    attended, log_total = lax.map(attend, by_head)
    mixed_heads = (
        jnp.transpose(attended, (1, 2, 0, 3)).reshape(row_count, HEADS * HEAD).astype(jnp.bfloat16)
    )
    middle = rows_float + jnp.dot(mixed_heads, full_out, preferred_element_type=jnp.float32)
    normal_two = normed(middle, gain_two).astype(jnp.bfloat16)
    gate_rows = jnp.dot(normal_two, full_gate, preferred_element_type=jnp.float32)
    upward = jnp.dot(normal_two, full_up, preferred_element_type=jnp.float32)
    activated = gelu_tanh(gate_rows)
    hidden = (activated * upward).astype(jnp.bfloat16)
    result = (middle + jnp.dot(hidden, full_down, preferred_element_type=jnp.float32)).astype(
        jnp.bfloat16
    )
    grad_float = grad_in.astype(jnp.float32)
    grad_down = contract_rows(hidden, grad_in)
    grad_hidden = against(grad_in, full_down)
    gelu_value, gelu_pull = jax.vjp(gelu_tanh, gate_rows)
    grad_gate_rows = gelu_pull(grad_hidden * upward)[0].astype(jnp.bfloat16)
    grad_up_rows = (grad_hidden * activated).astype(jnp.bfloat16)
    grad_gate = contract_rows(normal_two, grad_gate_rows)
    grad_up = contract_rows(normal_two, grad_up_rows)
    grad_two = against(grad_gate_rows, full_gate) + against(grad_up_rows, full_up)
    norm_value, norm_pull = jax.vjp(normed, middle, gain_two)
    grad_middle_norm, gain_two_grad = norm_pull(grad_two)
    grad_middle = grad_float + grad_middle_norm
    grad_middle_low = grad_middle.astype(jnp.bfloat16)
    grad_out = contract_rows(mixed_heads, grad_middle_low)
    grad_mixed = against(grad_middle_low, full_out).astype(jnp.bfloat16)
    grad_by_head = jnp.transpose(grad_mixed.reshape(MICRO, micro_rows, HEADS, HEAD), (2, 0, 1, 3))

    def attend_back(running, pieces):
        key_total, value_total = running
        query_head, grad_head, total_head = pieces
        scores = (
            jnp.einsum("mqd,mkd->mqk", query_head, all_keys, preferred_element_type=jnp.float32)
            * score_scale
        )
        soft_weights = jnp.where(allowed, jnp.exp(scores - total_head[..., None]), 0.0)
        value_total = value_total + jnp.einsum(
            "mqk,mqd->mkd",
            soft_weights.astype(jnp.bfloat16),
            grad_head,
            preferred_element_type=jnp.float32,
        )
        grad_soft = jnp.einsum(
            "mqd,mkd->mqk", grad_head, all_values, preferred_element_type=jnp.float32
        )
        row_delta = jnp.sum(grad_soft * soft_weights, axis=2, keepdims=True)
        grad_scores = (soft_weights * (grad_soft - row_delta)).astype(jnp.bfloat16)
        grad_query_head = (
            jnp.einsum("mqk,mkd->mqd", grad_scores, all_keys, preferred_element_type=jnp.float32)
            * score_scale
        )
        key_total = (
            key_total
            + jnp.einsum(
                "mqk,mqd->mkd", grad_scores, query_head, preferred_element_type=jnp.float32
            )
            * score_scale
        )
        return ((key_total, value_total), grad_query_head)

    zero_block = jnp.zeros((MICRO, (reach_steps + 1) * micro_rows, HEAD), jnp.float32)
    totals, grad_query_heads = lax.scan(
        attend_back, (zero_block, zero_block), (by_head, grad_by_head, log_total)
    )
    key_total, value_total = totals

    def piece_of(total, distance_step):
        begin_row = (reach_steps - distance_step) * micro_rows
        return total[:, begin_row : begin_row + micro_rows].reshape(row_count, HEAD)

    own_key = piece_of(key_total, 0)
    own_value = piece_of(value_total, 0)
    for distance_step in range(1, reach_steps + 1):
        returned_pair = (
            passed_along(
                piece_of(key_total, distance_step).astype(jnp.bfloat16),
                ("dp", "fsdp"),
                -distance_step,
            ).astype(jnp.float32),
            passed_along(
                piece_of(value_total, distance_step).astype(jnp.bfloat16),
                ("dp", "fsdp"),
                -distance_step,
            ).astype(jnp.float32),
        )
        own_key = own_key + returned_pair[0]
        own_value = own_value + returned_pair[1]
    grad_value_rows = own_value.astype(jnp.bfloat16)
    grad_query_rot = jnp.transpose(grad_query_heads, (1, 2, 0, 3)).reshape(row_count, HEADS, HEAD)
    grad_query_raw = (
        rotate(grad_query_rot, cosine[:, None, :], -sine_table[:, None, :])
        .reshape(row_count, HEADS * HEAD)
        .astype(jnp.bfloat16)
    )
    grad_key_raw = rotate(own_key, cosine, -sine_table).astype(jnp.bfloat16)
    grad_query = contract_rows(normal_one, grad_query_raw)
    grad_key = contract_rows(normal_one, grad_key_raw)
    grad_value = contract_rows(normal_one, grad_value_rows)
    grad_one = (
        against(grad_query_raw, full_query)
        + against(grad_key_raw, full_key)
        + against(grad_value_rows, full_value)
    )
    first_value, first_pull = jax.vjp(normed, rows_float, gain_one)
    grad_rows_norm, gain_one_grad = first_pull(grad_one)
    grad_rows = (grad_middle + grad_rows_norm).astype(jnp.bfloat16)
    grad_gains = jnp.stack([gain_one_grad, gain_two_grad])
    sectioned = (
        lax.psum_scatter(
            grad_query.astype(jnp.bfloat16), "fsdp", scatter_dimension=1, tiled=True
        ).astype(jnp.float32),
        lax.psum_scatter(
            grad_key.astype(jnp.bfloat16), "fsdp", scatter_dimension=1, tiled=True
        ).astype(jnp.float32),
        lax.psum_scatter(
            grad_value.astype(jnp.bfloat16), "fsdp", scatter_dimension=1, tiled=True
        ).astype(jnp.float32),
        lax.psum_scatter(
            grad_out.astype(jnp.bfloat16), "fsdp", scatter_dimension=0, tiled=True
        ).astype(jnp.float32),
        lax.psum_scatter(
            grad_gate.astype(jnp.bfloat16), "fsdp", scatter_dimension=1, tiled=True
        ).astype(jnp.float32),
        lax.psum_scatter(
            grad_up.astype(jnp.bfloat16), "fsdp", scatter_dimension=1, tiled=True
        ).astype(jnp.float32),
        lax.psum_scatter(
            grad_down.astype(jnp.bfloat16), "fsdp", scatter_dimension=0, tiled=True
        ).astype(jnp.float32),
        lax.psum_scatter(
            grad_gains.astype(jnp.bfloat16), "fsdp", scatter_dimension=0, tiled=True
        ).astype(jnp.float32),
    )
    reduced = (
        lax.psum_scatter(sectioned[0], "dp", scatter_dimension=0, tiled=True),
        lax.psum_scatter(sectioned[1], "dp", scatter_dimension=0, tiled=True),
        lax.psum_scatter(sectioned[2], "dp", scatter_dimension=0, tiled=True),
        lax.psum_scatter(sectioned[3], "dp", scatter_dimension=1, tiled=True),
        lax.psum_scatter(sectioned[4], "dp", scatter_dimension=0, tiled=True),
        lax.psum_scatter(sectioned[5], "dp", scatter_dimension=0, tiled=True),
        lax.psum_scatter(sectioned[6], "dp", scatter_dimension=1, tiled=True),
        lax.psum_scatter(sectioned[7], "dp", scatter_dimension=1, tiled=True),
    )
    returned = (
        lax.all_to_all(
            result[bucket_order].reshape(peer_count, per_peer, model_width),
            "dp",
            split_axis=0,
            concat_axis=0,
            tiled=True,
        ),
        lax.all_to_all(
            grad_rows[bucket_order].reshape(peer_count, per_peer, model_width),
            "dp",
            split_axis=0,
            concat_axis=0,
            tiled=True,
        ),
    )
    output = jnp.zeros_like(tokens).at[picked].set(returned[0].reshape(row_count, model_width))
    input_grad = jnp.zeros_like(tokens).at[picked].set(returned[1].reshape(row_count, model_width))
    return (
        output,
        input_grad,
        reduced[0],
        reduced[1],
        reduced[2],
        reduced[3],
        reduced[4],
        reduced[5],
        reduced[6],
        reduced[7],
    )


def solution(mesh):
    in_specs = (
        P(("dp", "fsdp"), None),
        P(("dp", "fsdp"), None),
        P(("dp", "fsdp")),
        P(),
        P("dp", "fsdp"),
        P("dp", "fsdp"),
        P("dp", "fsdp"),
        P("fsdp", "dp"),
        P("dp", "fsdp"),
        P("dp", "fsdp"),
        P("fsdp", "dp"),
        P("fsdp", "dp"),
    )
    out_specs = (
        P(("dp", "fsdp"), None),
        P(("dp", "fsdp"), None),
        P("dp", "fsdp"),
        P("dp", "fsdp"),
        P("dp", "fsdp"),
        P("fsdp", "dp"),
        P("dp", "fsdp"),
        P("dp", "fsdp"),
        P("fsdp", "dp"),
        P("fsdp", "dp"),
    )
    return jax.shard_map(
        per_device, mesh=mesh, in_specs=in_specs, out_specs=out_specs, check_vma=False
    )
```

profile of v0, /device:TPU:26, one launch (start us, length us, event | category | flops | bytes accessed | tf_op | source)
XLA Modules:
  0.0 2407.6 jit_solution(9116250006526048176)
XLA Ops:
  10.0 62.9 %all-gather.14.cloned.1.call-done = bf16[1536,768]{1,0:T(8,128)(2,1)} async-done(((bf16[96,768]{1,0:T(8,128)(2,1)}), bf16[1536,768]{1,0:T(8,128)(2,1)}) %all-gather.14.cloned.1.call-update) | async-done | bytes 2359312 | tf_op jit(solution)/shard_map/all_gather | solution.py:115
  73.5 63.3 %all-gather.18.cloned.1.call-done = bf16[768,1536]{0,1:T(8,128)(2,1)} async-done(((bf16[768,96]{0,1:T(8,128)(2,1)}), bf16[768,1536]{0,1:T(8,128)(2,1)}) %all-gather.18.cloned.1.call-update) | async-done | bytes 2359312 | tf_op jit(solution)/shard_map/all_gather | solution.py:118
  136.9 102.2 %all-gather.22.cloned.1.call-done = bf16[1536,2304]{1,0:T(8,128)(2,1)} async-done(((bf16[96,2304]{1,0:T(8,128)(2,1)}), bf16[1536,2304]{1,0:T(8,128)(2,1)}) %all-gather.22.cloned.1.call-update) | async-done | bytes 7077904 | tf_op jit(solution)/shard_map/all_gather | solution.py:119
  239.2 102.1 %all-gather.26.cloned.1.call-done = bf16[1536,2304]{1,0:T(8,128)(2,1)} async-done(((bf16[96,2304]{1,0:T(8,128)(2,1)}), bf16[1536,2304]{1,0:T(8,128)(2,1)}) %all-gather.26.cloned.1.call-update) | async-done | bytes 7077904 | tf_op jit(solution)/shard_map/all_gather | solution.py:120
  347.8 6.1 all-to-all-start
  357.0 34.6 %all-gather.2 = bf16[16,96,64]{1,2,0:T(8,128)(2,1)S(1)} all-gather(bf16[1,96,64]{1,2,0:T(8,128)(2,1)S(1)} %bitcast.275), channel_id=1, replica_groups=mesh['dp'=16,'fsdp'=2] {'dp'}, dimensions={0}, use_global_device_ids=true | all-gather | bytes 208896 | tf_op jit(solution)/shard_map/all_gather | solution.py:117
  399.9 12.8 all-to-all-start.1
  412.7 59.6 %all-reduce = bf16[1536]{0:T(1024)(128)(2,1)S(1)} all-reduce(bf16[1536]{0:T(1024)(128)(2,1)S(1)} %dynamic-update-slice), channel_id=1, replica_groups=mesh['dp'=16,'fsdp'=2] {'dp'}, use_global_device_ids=true, to_apply=%add | all-reduce | flops 1536 | bytes 6144
  478.7 8.6 all-to-all-start.3
  487.4 42.4 %all-gather.1 = bf16[16,96,64]{1,2,0:T(8,128)(2,1)S(1)} all-gather(bf16[1,96,64]{1,2,0:T(8,128)(2,1)S(1)} %bitcast.276), channel_id=1, replica_groups=mesh['dp'=16,'fsdp'=2] {'dp'}, dimensions={0}, use_global_device_ids=true | all-gather | bytes 208896 | tf_op jit(solution)/shard_map/all_gather | solution.py:116
  539.8 5.3 collective-permute-start.3
  593.7 43.9 %while.30 = (s32[]{:T(128)}, bf16[12,2,128,128]{3,2,1,0:T(8,128)(2,1)}, f32[12,2,128]{2,1,0:T(2,128)}, bf16[12,2,128,128]{3,2,1,0:T(8,128)(2,1)}, bf16[2,1152,12...) while((s32[]{:T(128)}, ...), condition=%wide.region_6.7_spmd.clone.clone, body=%wide.region_3.6_spmd.clone.sunk.clone | while | flops 154533632 | bytes 5227117 | solution.py:192
  646.2 10.7 fusion.98
  656.9 10.5 fusion.99
  667.4 13.3 multiply_convert_fusion.1
  680.7 17.3 fusion.100
  698.0 10.8 multiply_reduce_fusion.1
  710.5 4.6 convolution_convert_fusion.5
  717.5 143.2 %while.31 = (s32[]{:T(128)}, f32[2,1152,128]{2,1,0:T(8,128)S(1)}, f32[2,1152,128]{2,1,0:T(8,128)}, f32[12,2,128,128]{3,2,1,0:T(8,128)}, bf16[12,2,128,128]{3,2,1...) while((s32[]{:T(128)}, f32[2,1152,128]{2,1,0:T(8,128)S(1)}, ...), condition=%wide.region_12.13_spmd.clone.clone, body=%wide.region_10.12_spmd.clone.sunk.clone | while | flops 382828288 | bytes 21280492 | solution.py:255
  861.0 4.7 collective-permute-start.16
  865.8 5.5 collective-permute-start.17
  871.4 4.4 collective-permute-start.18
  875.9 6.0 collective-permute-start.19
  882.0 5.2 collective-permute-start.20
  888.9 4.6 collective-permute-start.21
  905.3 5.6 collective-permute-start.25
  947.9 8.8 convolution_convert_fusion.2
  956.8 10.2 convolution_convert_fusion.1
  968.2 9.0 convolution_convert_fusion
  978.5 4.7 fusion.101
  995.0 4.6 copy.146
  1004.0 13.7 convert_element_type.294
  1017.7 5.3 reduce-scatter.40.cloned.1.call-done
  1023.0 9.2 convert_element_type.296
  1032.3 17.4 reduce-scatter.44.cloned.1.call-done
  1049.7 10.8 copy.148
  1060.4 10.0 fusion.35
  1072.6 7.1 all-to-all-start.2
  1083.8 15.3 all-to-all-done.2
  1099.1 7.6 all-to-all-start.4
  1106.7 76.1 %reduce-scatter.54.cloned.1.call-done = f32[96,1]{1,0:T(8,128)} async-done(((f32[1536,1]{1,0:T(8,128)}), f32[96,1]{1,0:T(8,128)}) %reduce-scatter.54.cloned.1.call-update) | async-done | bytes 400
  1190.3 118.7 %reduce-scatter.46.cloned.1.call-done = f32[96,64]{1,0:T(8,128)} async-done(((f32[1536,64]{1,0:T(8,128)}), f32[96,64]{1,0:T(8,128)}) %reduce-scatter.46.cloned.1.call-update) | async-done | bytes 24592
  1310.5 124.5 %reduce-scatter.48.cloned.1.call-done = f32[96,64]{1,0:T(8,128)} async-done(((f32[1536,64]{1,0:T(8,128)}), f32[96,64]{1,0:T(8,128)}) %reduce-scatter.48.cloned.1.call-update) | async-done | bytes 24592
  1436.6 139.7 %reduce-scatter.50.cloned.1.call-done = f32[96,768]{1,0:T(8,128)} async-done(((f32[1536,768]{1,0:T(8,128)}), f32[96,768]{1,0:T(8,128)}) %reduce-scatter.50.cloned.1.call-update) | async-done | bytes 294928
  1576.3 142.6 %reduce-scatter.28.cloned.1.call-done = f32[96,768]{1,0:T(8,128)} async-done(((f32[1536,768]{1,0:T(8,128)}), f32[96,768]{1,0:T(8,128)}) %reduce-scatter.28.cloned.1.call-update) | async-done | bytes 294928 | tf_op jit(solution)/shard_map/reduce_scatter | solution.py:328
  1718.9 226.5 %reduce-scatter.38.cloned.1.call-done = f32[96,2304]{1,0:T(8,128)} async-done(((f32[1536,2304]{1,0:T(8,128)}), f32[96,2304]{1,0:T(8,128)}) %reduce-scatter.38.cloned.1.call-update) | async-done | bytes 884752 | tf_op jit(solution)/shard_map/reduce_scatter | solution.py:332
  1945.4 228.0 %reduce-scatter.42.cloned.1.call-done = f32[96,2304]{1,0:T(8,128)} async-done(((f32[1536,2304]{1,0:T(8,128)}), f32[96,2304]{1,0:T(8,128)}) %reduce-scatter.42.cloned.1.call-update) | async-done | bytes 884752 | tf_op jit(solution)/shard_map/reduce_scatter | solution.py:333
  2173.4 227.2 %reduce-scatter.52.cloned.1.call-done = f32[96,2304]{1,0:T(8,128)} async-done(((f32[1536,2304]{1,0:T(8,128)}), f32[96,2304]{1,0:T(8,128)}) %reduce-scatter.52.cloned.1.call-update) | async-done | bytes 884752
  (581 shorter events, 370.4 us)
Async XLA Ops:
  7.2 65.7 %all-gather.14.cloned.1.call-start = ((), (), s32[]{:S(2)}) async-start(), calls=%async_computation.20 | async-start | bytes 2506752 | tf_op jit(solution)/shard_map/all_gather | solution.py:115
  7.9 128.9 %all-gather.18.cloned.1.call-start = ((), (), s32[]{:S(2)}) async-start(), calls=%async_computation.22 | async-start | bytes 2506752 | tf_op jit(solution)/shard_map/all_gather | solution.py:118
  8.7 230.4 %all-gather.22.cloned.1.call-start = ((), (), s32[]{:S(2)}) async-start(), calls=%async_computation.24 | async-start | bytes 7520256 | tf_op jit(solution)/shard_map/all_gather | solution.py:119
  9.4 331.8 %all-gather.26.cloned.1.call-start = ((), (), s32[]{:S(2)}) async-start(), calls=%async_computation.26 | async-start | bytes 7520256 | tf_op jit(solution)/shard_map/all_gather | solution.py:120
  10.0 572.2 %all-gather.16.cloned.1.call-start = ((), (), s32[]{:S(2)}) async-start(), calls=%async_computation.21 | async-start | bytes 7077888 | tf_op jit(solution)/shard_map/all_gather | solution.py:125
  72.9 520.7 %all-gather.30.cloned.1.call-start = ((), (), s32[]{:S(2)}) async-start(), calls=%async_computation.28 | async-start | bytes 7520256 | tf_op jit(solution)/shard_map/all_gather | solution.py:121
  73.5 567.2 %all-gather.20.cloned.1.call-start = ((), (), s32[]{:S(2)}) async-start(), calls=%async_computation.23 | async-start | bytes 7077888 | tf_op jit(solution)/shard_map/all_gather | solution.py:128
  136.8 509.3 %all-gather.24.cloned.1.call-start = ((), (), s32[]{:S(2)}) async-start(), calls=%async_computation.25 | async-start | bytes 21233664 | tf_op jit(solution)/shard_map/all_gather | solution.py:129
  239.1 417.8 %all-gather.28.cloned.1.call-start = ((), (), s32[]{:S(2)}) async-start(), calls=%async_computation.27 | async-start | bytes 21233664 | tf_op jit(solution)/shard_map/all_gather | solution.py:130
  347.8 48.7 %all-to-all-start = ((s32[16,1,16]{2,1,0:T(1,128)}), s32[16,1,16]{2,1,0:T(1,128)S(1)}, u32[]{:S(2)}, u32[]{:S(2)}) async-start(s32[16,1,16]{2,1,0:T(1,128)} %all_to_all.18), calls=%async_computation | async-start | bytes 16384 | tf_op jit(solution)/shard_map/all_to_all | solution.py:94
  399.9 78.8 %all-to-all-start.1 = ((bf16[16,16,1536]{2,1,0:T(8,128)(2,1)}), bf16[16,16,1536]{2,1,0:T(8,128)(2,1)S(1)}, u32[]{:S(2)}, u32[]{:S(2)}) async-start(bf16[16,16,1536]{2,1,0:T(8,128)(2,1)} %bitcast.1), calls=%async_computation.1 | async-start | bytes 1572864 | tf_op jit(solution)/shard_map/all_to_all | solution.py:97
  478.7 78.0 %all-to-all-start.3 = ((bf16[16,16,1536]{2,1,0:T(8,128)(2,1)}), bf16[16,16,1536]{2,1,0:T(8,128)(2,1)S(1)}, u32[]{:S(2)}, u32[]{:S(2)}) async-start(bf16[16,16,1536]{2,1,0:T(8,128)(2,1)} %bitcast.36), calls=%async_computation.3 | async-start | bytes 1572864 | tf_op jit(solution)/shard_map/all_to_all | solution.py:104
  487.3 180.0 %all-gather.32.cloned.1.call-start = ((), (), s32[]{:S(2)}) async-start(), calls=%async_computation.29 | async-start | bytes 21233664 | tf_op jit(solution)/shard_map/all_gather | solution.py:131
  537.2 12.9 collective-permute-start.1
  538.5 13.7 collective-permute-start.2
  539.8 14.3 collective-permute-start.3
  545.1 14.9 collective-permute-start.4
  548.1 13.4 collective-permute-start.5
  550.0 13.5 collective-permute-start.6
  552.2 14.0 collective-permute-start.7
  554.1 14.8 collective-permute-start.8
  561.6 13.1 collective-permute-start.10
  563.6 14.1 collective-permute-start.11
  566.2 12.3 collective-permute-start.12
  593.6 396.9 %reduce-scatter.30.cloned.1.call-start = ((), (), s32[]{:S(2)}) async-start(), calls=%async_computation.32 | async-start | bytes 589824 | tf_op jit(solution)/shard_map/reduce_scatter | solution.py:305
  861.0 27.9 %collective-permute-start.16 = (bf16[256,128]{0,1:T(8,128)(2,1)S(1)}, bf16[256,128]{0,1:T(8,128)(2,1)S(1)}, u32[]{:S(2)}, u32[]{:S(2)}) collective-permute-start(bf16[256,128]{0,1:T(8,128)(2,1)S(1)} %copy.134), channel_id=1, source_target_pairs={{1,0},{2,1},{3,2},{4,3},{5,4},{6,5},{7,6},{8,7},{9,8},{10,9},{11,1... | collective-permute-start | bytes 196616 | tf_op jit(solution)/shard_map/ppermute | solution.py:19
  865.8 27.7 %collective-permute-start.17 = (bf16[256,128]{0,1:T(8,128)(2,1)S(1)}, bf16[256,128]{0,1:T(8,128)(2,1)S(1)}, u32[]{:S(2)}, u32[]{:S(2)}) collective-permute-start(bf16[256,128]{0,1:T(8,128)(2,1)S(1)} %copy.135), channel_id=1, source_target_pairs={{2,0},{3,1},{4,2},{5,3},{6,4},{7,5},{8,6},{9,7},{10,8},{11,9},{12,... | collective-permute-start | bytes 196616 | tf_op jit(solution)/shard_map/ppermute | solution.py:19
  871.4 24.6 %collective-permute-start.18 = (bf16[256,128]{0,1:T(8,128)(2,1)S(1)}, bf16[256,128]{0,1:T(8,128)(2,1)S(1)}, u32[]{:S(2)}, u32[]{:S(2)}) collective-permute-start(bf16[256,128]{0,1:T(8,128)(2,1)S(1)} %copy.136), channel_id=1, source_target_pairs={{3,0},{4,1},{5,2},{6,3},{7,4},{8,5},{9,6},{10,7},{11,8},{12,9},{13... | collective-permute-start | bytes 196616 | tf_op jit(solution)/shard_map/ppermute | solution.py:19
  875.9 23.8 collective-permute-start.19
  882.0 17.7 collective-permute-start.20
  902.5 90.1 %reduce-scatter.32.cloned.1.call-start = ((), (), s32[]{:S(2)}) async-start(), calls=%async_computation.33 | async-start | bytes 589824 | tf_op jit(solution)/shard_map/reduce_scatter | solution.py:308
  902.6 16.1 collective-permute-start.24
  905.3 15.1 collective-permute-start.25
  927.8 67.2 %reduce-scatter.34.cloned.1.call-start = ((), (), s32[]{:S(2)}) async-start(), calls=%async_computation.34 | async-start | bytes 7077888 | tf_op jit(solution)/shard_map/reduce_scatter | solution.py:311
  931.5 68.2 %reduce-scatter.26.cloned.1.call-start = ((), (), s32[]{:S(2)}) async-start(), calls=%async_computation.30 | async-start | bytes 7077888 | tf_op jit(solution)/shard_map/reduce_scatter | solution.py:302
  946.6 57.4 %reduce-scatter.36.cloned.1.call-start = ((), (), s32[]{:S(2)}) async-start(), calls=%async_computation.35 | async-start | bytes 21233664 | tf_op jit(solution)/shard_map/reduce_scatter | solution.py:314
  956.8 66.2 %reduce-scatter.40.cloned.1.call-start = ((), (), s32[]{:S(2)}) async-start(), calls=%async_computation.37 | async-start | bytes 21233664 | tf_op jit(solution)/shard_map/reduce_scatter | solution.py:317
  967.0 82.6 %reduce-scatter.44.cloned.1.call-start = ((), (), s32[]{:S(2)}) async-start(), calls=%async_computation.39 | async-start | bytes 21233664 | tf_op jit(solution)/shard_map/reduce_scatter | solution.py:320
  977.2 205.6 %reduce-scatter.54.cloned.1.call-start = ((), (), s32[]{:S(2)}) async-start(), calls=%async_computation.44 | async-start | bytes 835584
  990.4 318.6 %reduce-scatter.46.cloned.1.call-start = ((), (), s32[]{:S(2)}) async-start(), calls=%async_computation.40 | async-start | bytes 835584
  992.6 442.5 %reduce-scatter.48.cloned.1.call-start = ((), (), s32[]{:S(2)}) async-start(), calls=%async_computation.41 | async-start | bytes 835584
  994.7 581.6 %reduce-scatter.50.cloned.1.call-start = ((), (), s32[]{:S(2)}) async-start(), calls=%async_computation.42 | async-start | bytes 5013504
  999.6 719.3 %reduce-scatter.28.cloned.1.call-start = ((), (), s32[]{:S(2)}) async-start(), calls=%async_computation.31 | async-start | bytes 5013504 | tf_op jit(solution)/shard_map/reduce_scatter | solution.py:328
  1003.9 941.5 %reduce-scatter.38.cloned.1.call-start = ((), (), s32[]{:S(2)}) async-start(), calls=%async_computation.36 | async-start | bytes 15040512 | tf_op jit(solution)/shard_map/reduce_scatter | solution.py:332
  1017.7 1155.8 %reduce-scatter.42.cloned.1.call-start = ((), (), s32[]{:S(2)}) async-start(), calls=%async_computation.38 | async-start | bytes 15040512 | tf_op jit(solution)/shard_map/reduce_scatter | solution.py:333
  1032.2 1368.4 %reduce-scatter.52.cloned.1.call-start = ((), (), s32[]{:S(2)}) async-start(), calls=%async_computation.43 | async-start | bytes 15040512
  1072.6 26.4 %all-to-all-start.2 = ((bf16[16,16,1536]{2,1,0:T(8,128)(2,1)}), bf16[16,16,1536]{2,1,0:T(8,128)(2,1)}, u32[]{:S(2)}, u32[]{:S(2)}) async-start(bf16[16,16,1536]{2,1,0:T(8,128)(2,1)} %bitcast.239), calls=%async_computation.2 | async-start | bytes 1572864 | tf_op jit(solution)/shard_map/all_to_all | solution.py:338
  1099.1 88.4 %all-to-all-start.4 = ((bf16[16,16,1536]{2,1,0:T(8,128)(2,1)}), bf16[16,16,1536]{2,1,0:T(8,128)(2,1)S(1)}, u32[]{:S(2)}, u32[]{:S(2)}) async-start(bf16[16,16,1536]{2,1,0:T(8,128)(2,1)} %bitcast.61), calls=%async_computation.4 | async-start | bytes 1572864 | tf_op jit(solution)/shard_map/all_to_all | solution.py:345
  (96 other events, 2892.9 us)
Sparse Core Ops, SparseCore 0:
  10.8 62.0 all-gather.13
  75.7 61.0 all-gather.17
  139.6 99.4 all-gather.21
  241.8 99.4 all-gather.25
  342.6 14.7 all-gather.15
  360.1 109.4 all-gather.29
  471.2 16.2 all-gather.19
  489.0 27.5 all-gather.23
  518.2 27.5 all-gather.27
  593.8 37.7 all-gather.31
  902.6 10.1 reduce-scatter.29
  928.0 9.4 reduce-scatter.31
  939.8 13.7 reduce-scatter.33
  955.9 13.7 reduce-scatter.25
  971.8 24.4 reduce-scatter.35
  998.4 24.5 reduce-scatter.39
  1025.2 24.4 reduce-scatter.43
  1054.8 127.9 reduce-scatter.53
  1187.5 121.4 reduce-scatter.45
  1313.6 121.4 reduce-scatter.47
  1440.8 135.4 reduce-scatter.49
  1582.9 135.9 reduce-scatter.27
  1725.3 220.0 reduce-scatter.37
  1952.6 220.7 reduce-scatter.41
  2179.8 220.7 reduce-scatter.51
where the time goes:
time: 2420 us; the launch traced here: 2410 us
  waiting for transfers between devices  1660 us (69%)
  matrix products  259 us (11%)
  blocking collectives  145 us (6%)
  local copies, waits for them, and re-layouts  131 us (5%)
  starting transfers between devices  131 us (5%)
  other arithmetic  64.7 us (3%)
    unnamed x30, waiting for transfers between devices  690 us
    reduce_scatter x1, waiting for transfers between devices, per_device(): lax.psum_scatter(sectioned[5], 'dp', scatter_dimension=0, tiled=True)  228 us
    reduce_scatter x1, waiting for transfers between devices, per_device(): lax.psum_scatter(sectioned[4], 'dp', scatter_dimension=0, tiled=True)  226 us
    reduce_scatter x1, waiting for transfers between devices, per_device(): lax.psum_scatter(sectioned[0], 'dp', scatter_dimension=0, tiled=True)  143 us
    all_gather x1, waiting for transfers between devices, per_device(): lax.all_gather(w_gate, 'dp', axis=0, tiled=True)  102 us
    all_gather x1, waiting for transfers between devices, per_device(): lax.all_gather(w_up, 'dp', axis=0, tiled=True)  102 us
    ppermute x32, starting transfers between devices, passed_along(): return lax.ppermute(x, axis, pairs)  87.5 us
    all_gather x1, waiting for transfers between devices, per_device(): lax.all_gather(w_out, 'dp', axis=1, tiled=True)  63.3 us
  transfers between devices with their start and end apart: 62, of which 20 were waited for; matrix products, arithmetic and copies ran while one was open for 10% of the time, Pallas kernels for 0%

commit v1 on v0

--- a/solution.py
+++ b/solution.py
@@ -1,6 +1,10 @@
+import functools
+
 import jax
 import jax.numpy as jnp
 from jax import lax
+from jax.experimental import pallas as pl
+from jax.experimental.pallas import tpu as pltpu
 from jax.sharding import PartitionSpec as P
 
 HEADS = 12
@@ -11,6 +15,7 @@
 
 EPSILON = 1e-06
 NEGATIVE = -1e30
+VMEM_ASK = 62 * 2**20
 
 
 def passed_along(x, axis, by):
@@ -366,6 +371,1415 @@
     )
 
 
+MESH = pl.DeviceIdType.MESH
+BF16 = jnp.bfloat16
+F32 = jnp.float32
+PLANE = 4
+ANY = pl.BlockSpec(memory_space=pl.ANY)
+VM = pl.BlockSpec(memory_space=pltpu.VMEM)
+SM = pl.BlockSpec(memory_space=pltpu.SMEM)
+
+
+def mm(left, right):
+    return jnp.dot(left, right, preferred_element_type=F32)
+
+
+def mm_nt(left, right):
+    return lax.dot_general(left, right, (((1,), (1,)), ((), ())), preferred_element_type=F32)
+
+
+def mm_tn(left, right):
+    return lax.dot_general(left, right, (((0,), (0,)), ((), ())), preferred_element_type=F32)
+
+
+class Place:
+    def __init__(self, chips):
+        self.chips = chips
+        self.groups = chips // PLANE
+        self.d = lax.axis_index("dp")
+        self.f = lax.axis_index("fsdp")
+        self.other = 1 - self.f
+        self.g = self.d // PLANE
+        self.p = self.d % PLANE
+        self.x = self.p % 2
+        self.y = self.p // 2
+
+    def plane_pos(self, j):
+        return ((self.y + j // 2) % 2) * 2 + (self.x + j % 2) % 2
+
+    def plane_chip(self, j):
+        return self.g * PLANE + self.plane_pos(j)
+
+    def column_chip(self, k):
+        return ((self.g + k) % self.groups) * PLANE + self.p
+
+
+def greet_all(place):
+    barrier = pltpu.get_barrier_semaphore()
+    total = place.chips * 2
+    me = place.d * 2 + place.f
+
+    def signal(k, carry):
+        to = (me + k) % total
+        pl.semaphore_signal(barrier, inc=1, device_id=(to // 2, to % 2), device_id_type=MESH)
+        return carry
+
+    lax.fori_loop(1, total, signal, 0)
+    pl.semaphore_wait(barrier, total - 1)
+
+
+class Sent:
+    def __init__(self):
+        self.copies = []
+
+    def remote(self, src, dst, send_sem, recv_sem, device):
+        copy = pltpu.make_async_remote_copy(
+            src_ref=src,
+            dst_ref=dst,
+            send_sem=send_sem,
+            recv_sem=recv_sem,
+            device_id=device,
+            device_id_type=MESH,
+        )
+        copy.start()
+        self.copies.append(copy)
+
+    def finish(self):
+        for copy in self.copies:
+            copy.wait_send()
+        self.copies = []
+
+
+def arrived(ref, sem):
+    pltpu.make_async_copy(ref, ref, sem).wait()
+
+
+def iota(shape, dim):
+    return lax.broadcasted_iota(jnp.int32, shape, dim)
+
+
+def gain_spread(width, share):
+    column = iota((128, width), 1).astype(F32)
+    inside = column - jnp.floor((column + 0.5) * (1.0 / share)) * share
+    row = iota((128, width), 0).astype(F32)
+    return (inside == row).astype(BF16)
+
+
+def own_stretch(chips, width, share):
+    row = iota((chips, width), 0)
+    column = iota((chips, width), 1)
+    return (column >= row * share) & (column < row * share + share)
+
+
+def gain_row(kvg_ref, which, chips, width, share):
+    block = kvg_ref[which, :, share : share + 16, :].astype(F32)[:, 0, :].astype(BF16)
+    spread = mm(block, gain_spread(width, share))
+    return jnp.sum(jnp.where(own_stretch(chips, width, share), spread, 0.0), axis=0, keepdims=True)
+
+
+def gather_kernel(
+    chips,
+    deal_ref,
+    deal_col_ref,
+    tokens_ref,
+    cot_ref,
+    wq_ref,
+    wot_ref,
+    kvg_ref,
+    gate_ref,
+    up_ref,
+    down_ref,
+    full_q,
+    full_ot,
+    full_kvg,
+    full_three,
+    rows_out,
+    pg_all,
+    take_ref,
+    place_ref,
+    deal_all,
+    give,
+    got,
+    deal_send,
+    deal_recv,
+    row_send,
+    row_recv,
+    attn_send,
+    attn_recv,
+    fan_send,
+    kv_sems,
+    three_send,
+    three_recv,
+    relay_send,
+    relay_recv,
+    own_sems,
+    pg_send,
+    pg_recv,
+    local_sems,
+):
+    place = Place(chips)
+    d, f, other = place.d, place.f, place.other
+    rows, width = tokens_ref.shape
+    share = wq_ref.shape[0]
+    half = share // 2
+    per = rows // chips
+    part = gate_ref.shape[1] // 2
+    sent = Sent()
+    greet_all(place)
+
+    deal_all[d] = deal_ref[...]
+    for k in range(1, chips):
+        to = (d + k) % chips
+        sent.remote(
+            deal_all.at[d], deal_all.at[d], deal_send.at[k], deal_recv.at[d], (to, f)
+        )
+
+    def attn_slices(s):
+        band = pl.ds(pl.multiple_of(s * share, 16), share)
+        return (full_q.at[band], full_ot.at[band], full_kvg.at[f, s])
+
+    mine = attn_slices(d)
+    sources = (wq_ref, wot_ref, kvg_ref)
+    for a in range(3):
+        for k in range(1, place.groups):
+            sent.remote(
+                sources[a], mine[a], attn_send.at[a, k], attn_recv.at[a, d], (place.column_chip(k), f)
+            )
+    locals_ = [pltpu.make_async_copy(sources[a], mine[a], local_sems.at[a]) for a in range(3)]
+    for copy in locals_:
+        copy.start()
+    for a in range(3):
+        for j in range(1, PLANE):
+            sent.remote(
+                sources[a],
+                mine[a],
+                fan_send.at[a, 0, j],
+                attn_recv.at[a, d],
+                (place.plane_chip(j), f),
+            )
+
+    mats = (gate_ref, up_ref, down_ref)
+
+    three_copies = []
+    for k in range(place.groups):
+        for b in range(2):
+            to_x = (place.x + b) % 2
+            chip = ((place.g + k) % place.groups) * PLANE + 2 * f + to_x
+            slot = 2 * k + b
+            for core in range(2):
+                for a in range(3):
+                    src = mats[a].at[
+                        pl.ds(half * core, half), pl.ds(pl.multiple_of(part * to_x, 128), part)
+                    ]
+                    dst = full_three.at[a, pl.ds(pl.multiple_of(d * share + half * core, 16), half)]
+                    copy = pltpu.make_async_remote_copy(
+                        src_ref=src,
+                        dst_ref=dst,
+                        send_sem=three_send.at[a, slot, core],
+                        recv_sem=three_recv.at[a, d],
+                        device_id=(chip, core),
+                        device_id_type=MESH,
+                    )
+                    three_copies.append((slot, copy))
+    for slot, copy in three_copies:
+        if slot == 0:
+            pl.when(place.y != f)(copy.start)
+        else:
+            copy.start()
+
+    def own_parts():
+        band = pl.ds(pl.multiple_of(d * share, 16), share)
+        to = []
+        for a in range(3):
+            src = mats[a].at[:, pl.ds(pl.multiple_of(part * place.x, 128), part)]
+            to.append((src, full_three.at[a, band]))
+        return to
+
+    def own_local():
+        return [
+            pltpu.make_async_copy(src, dst, local_sems.at[3 + a])
+            for a, (src, dst) in enumerate(own_parts())
+        ]
+
+    def own_remote():
+        return [
+            pltpu.make_async_remote_copy(
+                src_ref=src,
+                dst_ref=dst,
+                send_sem=own_sems.at[0, a],
+                recv_sem=own_sems.at[1, a],
+                device_id=(d, other),
+                device_id_type=MESH,
+            )
+            for a, (src, dst) in enumerate(own_parts())
+        ]
+
+    @pl.when(place.y == f)
+    def _():
+        for copy in own_local() + own_remote():
+            copy.start()
+
+    for k in range(1, chips):
+        arrived(deal_all.at[(d + k) % chips], deal_recv.at[(d + k) % chips])
+    deals = deal_all[:, 0, :]
+    chip_bits = (2 * rows).bit_length() - 1
+    wants = lax.shift_right_logical(deals, chip_bits) == d
+    offset = deals & (rows - 1)
+    earlier = (iota((rows, rows), 0) < iota((rows, rows), 1)).astype(BF16)
+    rank = mm(wants.astype(F32).astype(BF16), earlier)
+    for j in range(chips):
+        hit = wants[j : j + 1, :] & (rank[j : j + 1, :] == iota((per, rows), 0).astype(F32))
+        index = jnp.sum(jnp.where(hit, offset[j : j + 1, :], 0), axis=1, keepdims=True)
+        take_ref[j * per : (j + 1) * per, :] = (index == iota((per, rows), 1)).astype(F32).astype(BF16)
+    give[:, :width] = mm(take_ref[...], tokens_ref[...]).astype(BF16)
+    give[:, width:] = mm(take_ref[...], cot_ref[...]).astype(BF16)
+
+    def block(k):
+        return pl.ds(pl.multiple_of(k * per, per), per)
+
+    for k in range(1, chips):
+        to = (d + k) % chips
+        sent.remote(give.at[block(to)], got.at[block(d)], row_send.at[k], row_recv.at[d], (to, f))
+    got[block(d), :] = give[block(d), :]
+
+    for k in range(1, place.groups):
+        s = place.column_chip(k)
+        piece = attn_slices(s)
+        for a in range(3):
+            arrived(piece[a], attn_recv.at[a, s])
+            for j in range(1, PLANE):
+                sent.remote(
+                    piece[a],
+                    piece[a],
+                    fan_send.at[a, k, j],
+                    attn_recv.at[a, s],
+                    (place.plane_chip(j), f),
+                )
+
+    source_col = lax.shift_right_logical(deal_col_ref[...], chip_bits)
+    source_row = lax.shift_right_logical(deal_ref[0:1, :], chip_bits)
+    same = (source_col == source_row) & (iota((rows, rows), 1) < iota((rows, rows), 0))
+    order = jnp.sum(same.astype(F32), axis=1, keepdims=True).astype(jnp.int32)
+    where_from = source_col * per + order
+    place_ref[...] = (where_from == iota((rows, rows), 1)).astype(F32).astype(BF16)
+    for k in range(1, chips):
+        s = (d + k) % chips
+        arrived(got.at[block(s)], row_recv.at[s])
+    rows_out[...] = mm(place_ref[...], got[:, :width]).astype(BF16)
+    pg_all[place.p] = mm(place_ref[...], got[:, width:]).astype(BF16)
+    for j in range(1, PLANE):
+        sent.remote(
+            pg_all.at[place.p],
+            pg_all.at[place.p],
+            pg_send.at[j],
+            pg_recv.at[place.p],
+            (place.plane_chip(j), f),
+        )
+
+    for k in range(place.groups):
+        for j in range(PLANE):
+            s = ((place.g + k) % place.groups) * PLANE + place.plane_pos(j)
+            if k == 0 and j == 0:
+                continue
+            band = pl.ds(pl.multiple_of(s * share + half * f, 16), half)
+            for a in range(3):
+                piece = full_three.at[a, band]
+                arrived(piece, three_recv.at[a, s])
+                sent.remote(piece, piece, relay_send.at[a, s], relay_recv.at[a, s], (d, other))
+    for k in range(place.groups):
+        for j in range(1, PLANE):
+            s = ((place.g + k) % place.groups) * PLANE + place.plane_pos(j)
+            piece = attn_slices(s)
+            for a in range(3):
+                arrived(piece[a], attn_recv.at[a, s])
+    for copy in locals_:
+        copy.wait()
+    sent.remote(full_kvg.at[f], full_kvg.at[f], kv_sems.at[0], kv_sems.at[1], (d, other))
+    for j in range(1, PLANE):
+        pos = place.plane_pos(j)
+        arrived(pg_all.at[pos], pg_recv.at[pos])
+    for k in range(place.groups):
+        for j in range(PLANE):
+            s = ((place.g + k) % place.groups) * PLANE + place.plane_pos(j)
+            if k == 0 and j == 0:
+                continue
+            band = pl.ds(pl.multiple_of(s * share + half * other, 16), half)
+            for a in range(3):
+                arrived(full_three.at[a, band], relay_recv.at[a, s])
+
+    @pl.when(place.y == f)
+    def _():
+        for copy in own_local():
+            copy.wait()
+        for copy in own_remote():
+            copy.wait_send()
+
+    @pl.when(place.y != f)
+    def _():
+        for copy in own_remote():
+            copy.wait_recv()
+
+    arrived(full_kvg.at[other], kv_sems.at[1])
+    for slot, copy in three_copies:
+        if slot == 0:
+            pl.when(place.y != f)(copy.wait_send)
+        else:
+            copy.wait_send()
+    sent.finish()
+
+
+def gather(chips, deal, tokens, cotangent, wq, wot, kvg, gate, up, down):
+    rows, width = tokens.shape
+    share = wq.shape[0]
+    groups = chips // PLANE
+    part = gate.shape[1] // 2
+    dma = pltpu.SemaphoreType.DMA
+    deal_rows = jnp.broadcast_to(deal[None, :], (8, rows))
+    deal_col = jnp.broadcast_to(deal[:, None], (rows, rows))
+    return pl.pallas_call(
+        functools.partial(gather_kernel, chips),
+        out_shape=(
+            jax.ShapeDtypeStruct((width, wq.shape[1]), BF16),
+            jax.ShapeDtypeStruct((width, wq.shape[1]), BF16),
+            jax.ShapeDtypeStruct((2, chips) + kvg.shape, BF16),
+            jax.ShapeDtypeStruct((3, width, part), BF16),
+            jax.ShapeDtypeStruct((rows, width), BF16),
+            jax.ShapeDtypeStruct((PLANE, rows, width), BF16),
+            jax.ShapeDtypeStruct((rows, rows), BF16),
+            jax.ShapeDtypeStruct((rows, rows), BF16),
+        ),
+        in_specs=[VM] * 4 + [ANY] * 6,
+        out_specs=(ANY, ANY, ANY, ANY, VM, VM, VM, VM),
+        scratch_shapes=[
+            pltpu.VMEM((chips, 8, rows), jnp.int32),
+            pltpu.VMEM((rows, 2 * width), BF16),
+            pltpu.VMEM((rows, 2 * width), BF16),
+            dma((chips,)),
+            dma((chips,)),
+            dma((chips,)),
+            dma((chips,)),
+            dma((3, groups)),
+            dma((3, chips)),
+            dma((3, groups, PLANE)),
+            dma((2,)),
+            dma((3, 2 * groups, 2)),
+            dma((3, chips)),
+            dma((3, chips)),
+            dma((3, chips)),
+            dma((2, 3)),
+            dma((PLANE,)),
+            dma((PLANE,)),
+            dma((6,)),
+        ],
+        compiler_params=pltpu.CompilerParams(
+            collective_id=0, has_side_effects=True, vmem_limit_bytes=VMEM_ASK
+        ),
+        name="gather_weights_and_rows",
+    )(deal_rows, deal_col, tokens, cotangent, wq, wot, kvg, gate, up, down)
+
+
+def rms_scale(values):
+    return lax.rsqrt(jnp.mean(values * values, axis=-1, keepdims=True) + EPSILON)
+
+
+def turned(values, cosine, sine):
+    return values * cosine + pltpu.roll(values, HEAD // 2, 1) * sine
+
+
+def halves_in(first, second):
+    front = iota(first.shape, 1) < HEAD // 2
+    return (
+        jnp.where(front, first, pltpu.roll(second, HEAD // 2, 1)),
+        jnp.where(front, pltpu.roll(first, HEAD // 2, 1), second),
+    )
+
+
+def attention_kernel(
+    chips,
+    reach,
+    first_ref,
+    rows_ref,
+    wq_ref,
+    wot_ref,
+    kvg_ref,
+    cos_ref,
+    sin_ref,
+    n1_ref,
+    qs_ref,
+    kv_ref,
+    probs_ref,
+    mixed_ref,
+    middle_ref,
+    n2_ref,
+    bias_ref,
+    branch_out,
+    branch_in,
+    n1_sems,
+    kv_send,
+    kv_recv,
+    branch_sems,
+):
+    place = Place(chips)
+    d, f, other = place.d, place.f, place.other
+    rows, width = rows_ref.shape
+    micro = rows // MICRO
+    heads = wq_ref.shape[1] // HEAD
+    share = width // chips
+    slots = 2 * reach + 2
+    span = (2 * reach + 1) * micro
+    sent = Sent()
+    greet_all(place)
+
+    row_values = rows_ref[...].astype(F32)
+    gain_one = gain_row(kvg_ref, 0, chips, width, share)
+    n1_ref[f] = (row_values * rms_scale(row_values) * gain_one).astype(BF16)
+    sent.remote(n1_ref.at[f], n1_ref.at[f], n1_sems.at[0], n1_sems.at[1], (d, other))
+
+    kvw = [kvg_ref[i, :, 0:share, :].reshape(width, HEAD) for i in range(2)]
+    raw = [mm(n1_ref[f], kvw[i]) for i in range(2)]
+    key_raw, value_raw = halves_in(raw[0], raw[1])
+    for m in range(MICRO):
+        hm = 2 * f + m
+        band = slice(m * micro, (m + 1) * micro)
+        key = turned(key_raw[band], cos_ref[hm], sin_ref[hm])
+        kv_ref[m, 2 * reach + f, :, 0:HEAD] = key.astype(BF16)
+        kv_ref[m, 2 * reach + f, :, HEAD:] = value_raw[band].astype(BF16)
+    own_kv = kv_ref.at[:, 2 * reach + f]
+
+    def kv_copy(j, core):
+        slot = 2 * reach + f - 2 * j
+        return pltpu.make_async_remote_copy(
+            src_ref=own_kv,
+            dst_ref=kv_ref.at[:, slot],
+            send_sem=kv_send.at[j, core],
+            recv_sem=kv_recv.at[slot],
+            device_id=(d + j, core),
+            device_id_type=MESH,
+        )
+
+    sent.remote(
+        own_kv, own_kv, kv_send.at[0, 0], kv_recv.at[2 * reach + f], (d, other)
+    )
+    for j in range(1, reach + 1):
+
+        @pl.when(d + j < chips)
+        def _():
+            for core in range(2):
+                kv_copy(j, core).start()
+
+        @pl.when(d - j < 0)
+        def _():
+            for core in range(2):
+                kv_ref[:, 2 * reach - 2 * j + core] = jnp.zeros((MICRO, micro, 2 * HEAD), BF16)
+
+    def project(h):
+        raw_q = mm(n1_ref[h], wq_ref[...])
+        for m in range(MICRO):
+            hm = 2 * h + m
+            cosine, sine = cos_ref[hm], sin_ref[hm]
+            for i in range(heads):
+                one = raw_q[m * micro : (m + 1) * micro, i * HEAD : (i + 1) * HEAD]
+                qs_ref[hm, i * micro : (i + 1) * micro, :] = turned(one, cosine, sine).astype(BF16)
+
+    project(f)
+    arrived(n1_ref.at[other], n1_sems.at[1])
+    project(other)
+
+    def make_bias(hm, carry):
+        h, m = hm // 2, hm % 2
+        first = first_ref[m]
+        query = (2 * d + h) * micro + iota((span, micro), 1)
+        key = (2 * d + h - 2 * reach) * micro + iota((span, micro), 0)
+        allowed = (
+            (jnp.where(query >= first, 1, 0) == jnp.where(key >= first, 1, 0))
+            & (key >= 0)
+            & (key <= query)
+            & (query - key < WINDOW)
+        )
+        bias_ref[hm] = jnp.where(allowed, 0.0, NEGATIVE)
+        return carry
+
+    lax.fori_loop(0, 4, make_bias, 0)
+    arrived(kv_ref.at[:, 2 * reach + other], kv_recv.at[2 * reach + other])
+    for j in range(1, reach + 1):
+
+        @pl.when(d - j >= 0)
+        def _():
+            for core in range(2):
+                slot = 2 * reach - 2 * j + core
+                arrived(kv_ref.at[:, slot], kv_recv.at[slot])
+
+    score_scale = HEAD ** (-0.5)
+
+    def attend(hm, carry):
+        h, m = hm // 2, hm % 2
+        keys = kv_ref[m, pl.ds(h, 2 * reach + 1), :, 0:HEAD].reshape(span, HEAD)
+        values_t = kv_ref[m, pl.ds(h, 2 * reach + 1), :, HEAD:].reshape(span, HEAD).T
+        for pair in range(heads // 2):
+            band = slice(pair * 2 * micro, (pair + 1) * 2 * micro)
+            bias = bias_ref[hm]
+            scores = mm_nt(keys, qs_ref[hm, band, :]) * score_scale + jnp.concatenate(
+                [bias, bias], axis=1
+            )
+            exp_scores = jnp.exp(scores - jnp.max(scores, axis=0, keepdims=True))
+            total = jnp.sum(exp_scores, axis=0, keepdims=True)
+            probs = (exp_scores * (1.0 / total)).astype(BF16)
+            probs_ref[hm, :, band] = probs
+            out_t = mm(values_t, probs)
+            for i in range(2):
+                one = out_t[:, i * micro : (i + 1) * micro].T
+                head = pair * 2 + i
+                mixed_ref[hm, :, head * HEAD : (head + 1) * HEAD] = one.astype(BF16)
+        return carry
+
+    lax.fori_loop(0, 4, attend, 0)
+
+    def branch(h):
+        return mm_nt(mixed_ref[pl.ds(2 * h, 2)].reshape(rows, heads * HEAD), wot_ref[...])
+
+    branch_out[...] = branch(other).astype(BF16)
+    sent.remote(branch_out, branch_in, branch_sems.at[0], branch_sems.at[1], (d, other))
+    own = branch(f)
+    arrived(branch_in, branch_sems.at[1])
+    middle = row_values + own + branch_in[...].astype(F32)
+    middle_ref[...] = middle
+    gain_two = gain_row(kvg_ref, 1, chips, width, share)
+    n2_ref[...] = (middle * rms_scale(middle) * gain_two).astype(BF16)
+
+    for j in range(1, reach + 1):
+
+        @pl.when(d + j < chips)
+        def _():
+            for core in range(2):
+                kv_copy(j, core).wait_send()
+
+    sent.finish()
+
+
+def attention(chips, reach, first_len, rows_in, wq, wot, kvg, cosine, sine):
+    rows, width = rows_in.shape
+    micro = rows // MICRO
+    heads = wq.shape[1] // HEAD
+    slots = 2 * reach + 2
+    span = (2 * reach + 1) * micro
+    dma = pltpu.SemaphoreType.DMA
+    shape = jax.ShapeDtypeStruct
+    return pl.pallas_call(
+        functools.partial(attention_kernel, chips, reach),
+        out_shape=(
+            shape((2, rows, width), BF16),
+            shape((4, heads * micro, HEAD), BF16),
+            shape((MICRO, slots, micro, 2 * HEAD), BF16),
+            shape((4, span, heads * micro), BF16),
+            shape((4, micro, heads * HEAD), BF16),
+            shape((rows, width), F32),
+            shape((rows, width), BF16),
+        ),
+        in_specs=[SM] + [VM] * 6,
+        out_specs=(VM,) * 7,
+        scratch_shapes=[
+            pltpu.VMEM((4, span, micro), F32),
+            pltpu.VMEM((rows, width), BF16),
+            pltpu.VMEM((rows, width), BF16),
+            dma((2,)),
+            dma((reach + 1, 2)),
+            dma((slots,)),
+            dma((2,)),
+        ],
+        compiler_params=pltpu.CompilerParams(
+            collective_id=1, has_side_effects=True, vmem_limit_bytes=VMEM_ASK
+        ),
+        name="attention_forward",
+    )(first_len, rows_in, wq, wot, kvg, cosine, sine)
+
+
+def mlp_kernel(
+    chips,
+    n2_ref,
+    middle_ref,
+    pg_ref,
+    three_ref,
+    out_ref,
+    two_ref,
+    grads_ref,
+    n2_all,
+    turned_ref,
+    hidden_ref,
+    gate_rows_ref,
+    up_rows_ref,
+    two_give,
+    two_got,
+    out_give,
+    out_got,
+    n2_send,
+    n2_recv,
+    two_send,
+    two_recv,
+    out_send,
+    out_recv,
+):
+    place = Place(chips)
+    f, p = place.f, place.p
+    rows, width = n2_ref.shape
+    part = three_ref.shape[2]
+    greet_all(place)
+    sent = Sent()
+    n2_all[p] = n2_ref[...]
+    for j in range(1, PLANE):
+        sent.remote(
+            n2_all.at[p], n2_all.at[p], n2_send.at[j], n2_recv.at[p], (place.plane_chip(j), f)
+        )
+
+    def two_copy(j):
+        return pltpu.make_async_remote_copy(
+            src_ref=two_give.at[j - 1],
+            dst_ref=two_got.at[j - 1],
+            send_sem=two_send.at[j],
+            recv_sem=two_recv.at[j],
+            device_id=(place.plane_chip(j), f),
+            device_id_type=MESH,
+        )
+
+    def out_copy(j):
+        return pltpu.make_async_remote_copy(
+            src_ref=out_give.at[j - 1],
+            dst_ref=out_got.at[j - 1],
+            send_sem=out_send.at[j],
+            recv_sem=out_recv.at[j],
+            device_id=(place.plane_chip(j), f),
+            device_id_type=MESH,
+        )
+
+    curve = 0.7978845608028654
+    cubic = 0.044715
+
+    def one_block(j, carry):
+        pos = place.plane_pos(j)
+
+        @pl.when(j > 0)
+        def _():
+            arrived(n2_all.at[pos], n2_recv.at[pos])
+
+        x = n2_all[pos]
+        gate = mm(x, three_ref[0])
+        upward = mm(x, three_ref[1])
+        grad_hidden = mm(pg_ref[pos], three_ref[2])
+        square = gate * gate
+        tanh = jnp.tanh(curve * gate * (1.0 + cubic * square))
+        activated = 0.5 * gate * (1.0 + tanh)
+        slope = 0.5 * (1.0 + tanh) + (0.5 * curve) * gate * (1.0 - tanh * tanh) * (
+            1.0 + (3.0 * cubic) * square
+        )
+        band = pl.ds(pl.multiple_of(pos * rows, rows), rows)
+        hidden_ref[band, :] = (activated * upward).astype(BF16)
+        gate_rows_ref[band, :] = (grad_hidden * upward * slope).astype(BF16)
+        up_rows_ref[band, :] = (grad_hidden * activated).astype(BF16)
+        back = mm_nt(gate_rows_ref[band, :], three_ref[0]) + mm_nt(up_rows_ref[band, :], three_ref[1])
+
+        @pl.when(j > 0)
+        def _():
+            two_give[j - 1] = back.astype(BF16)
+            two_copy(j).start()
+
+        @pl.when(j == 0)
+        def _():
+            two_ref[...] = back
+
+        return carry
+
+    lax.fori_loop(0, PLANE, one_block, 0)
+
+    def out_step(j):
+        pos = place.plane_pos(j)
+        band = pl.ds(pl.multiple_of(pos * rows, rows), rows)
+        return pos, mm_nt(hidden_ref[band, :], three_ref[2])
+
+    def send_out(j, carry):
+        pos, piece = out_step(j)
+        out_give[j - 1] = piece.astype(BF16)
+        out_copy(j).start()
+        return carry
+
+    lax.fori_loop(1, PLANE, send_out, 0)
+    own_out = middle_ref[...] + out_step(0)[1]
+
+    tile = rows
+    tiles = width // tile
+
+    def turn(source, index):
+        def step(i, carry):
+            at = pl.ds(pl.multiple_of(i * rows, rows), rows)
+            turned_ref[:, at] = source[i].T
+            return carry
+
+        lax.fori_loop(0, PLANE, step, 0)
+
+    def weight_grad(index, right):
+        def step(i, carry):
+            at = pl.ds(pl.multiple_of(i * tile, tile), tile)
+            grads_ref[index, at, :] = mm(turned_ref[at, :], right[...]).astype(BF16)
+            return carry
+
+        lax.fori_loop(0, tiles, step, 0)
+
+    turn(pg_ref, 0)
+    weight_grad(2, hidden_ref)
+    turn(n2_all, 1)
+    weight_grad(0, gate_rows_ref)
+    weight_grad(1, up_rows_ref)
+
+    for j in range(1, PLANE):
+        arrived(two_got.at[j - 1], two_recv.at[j])
+        two_ref[...] = two_ref[...] + two_got[j - 1].astype(F32)
+    for j in range(1, PLANE):
+        arrived(out_got.at[j - 1], out_recv.at[j])
+        own_out = own_out + out_got[j - 1].astype(F32)
+    out_ref[...] = own_out.astype(BF16)
+    for j in range(1, PLANE):
+        two_copy(j).wait_send()
+        out_copy(j).wait_send()
+    sent.finish()
+
+
+def mlp(chips, n2, middle, pg_all, three):
+    rows, width = n2.shape
+    part = three.shape[2]
+    dma = pltpu.SemaphoreType.DMA
+    shape = jax.ShapeDtypeStruct
+    wide = PLANE * rows
+    return pl.pallas_call(
+        functools.partial(mlp_kernel, chips),
+        out_shape=(
+            shape((rows, width), BF16),
+            shape((rows, width), F32),
+            shape((3, width, part), BF16),
+        ),
+        in_specs=[VM] * 4,
+        out_specs=(VM,) * 3,
+        scratch_shapes=[
+            pltpu.VMEM((PLANE, rows, width), BF16),
+            pltpu.VMEM((width, wide), BF16),
+            pltpu.VMEM((wide, part), BF16),
+            pltpu.VMEM((wide, part), BF16),
+            pltpu.VMEM((wide, part), BF16),
+        ]
+        + [pltpu.VMEM((PLANE - 1, rows, width), BF16)] * 4
+        + [dma((PLANE,))] * 6,
+        compiler_params=pltpu.CompilerParams(
+            collective_id=2, has_side_effects=True, vmem_limit_bytes=VMEM_ASK
+        ),
+        name="mlp_both_ways",
+    )(n2, middle, pg_all, three)
+
+
+def norm_back(values, gain, grad):
+    scale = rms_scale(values)
+    unit = values * scale
+    lifted = grad * gain
+    gain_grad = jnp.sum(grad * unit, axis=0, keepdims=True)
+    back = scale * (lifted - unit * jnp.mean(lifted * unit, axis=-1, keepdims=True))
+    return back, gain_grad
+
+
+def attention_back_kernel(
+    chips,
+    reach,
+    rows_ref,
+    pg_ref,
+    middle_ref,
+    two_ref,
+    n1_ref,
+    qs_ref,
+    kv_ref,
+    probs_ref,
+    mixed_ref,
+    wq_ref,
+    wot_ref,
+    kvg_ref,
+    cos_ref,
+    sin_ref,
+    grad_rows_ref,
+    gq_ref,
+    got_ref,
+    gkvg_ref,
+    low_ref,
+    lows_t,
+    mixed_rows,
+    grad_mixed,
+    grad_q,
+    kv_total,
+    kv_give,
+    kv_got,
+    one_out,
+    one_in,
+    low_sems,
+    kv_send,
+    kv_recv,
+    one_sems,
+):
+    place = Place(chips)
+    d, f, other = place.d, place.f, place.other
+    rows, width = rows_ref.shape
+    micro = rows // MICRO
+    heads = wq_ref.shape[1] // HEAD
+    share = width // chips
+    slots = 2 * reach + 2
+    span = (2 * reach + 1) * micro
+    sent = Sent()
+    greet_all(place)
+
+    gain_two = gain_row(kvg_ref, 1, chips, width, share)
+    back, gain_two_grad = norm_back(middle_ref[...], gain_two, two_ref[...])
+    grad_middle = pg_ref[...].astype(F32) + back
+    low_ref[f] = grad_middle.astype(BF16)
+    sent.remote(low_ref.at[f], low_ref.at[f], low_sems.at[0], low_sems.at[1], (d, other))
+    kv_total[...] = jnp.zeros_like(kv_total)
+
+    def mix_back(h):
+        grads = mm(low_ref[h], wot_ref[...])
+        for m in range(MICRO):
+            for i in range(heads):
+                grad_mixed[2 * h + m, i * micro : (i + 1) * micro, :] = grads[
+                    m * micro : (m + 1) * micro, i * HEAD : (i + 1) * HEAD
+                ].astype(BF16)
+
+    mix_back(f)
+    arrived(low_ref.at[other], low_sems.at[1])
+    mix_back(other)
+
+    score_scale = HEAD ** (-0.5)
+
+    def attend_back(hm, carry):
+        h, m = hm // 2, hm % 2
+        at = pl.ds(h, 2 * reach + 1)
+        keys = kv_ref[m, at, :, 0:HEAD].reshape(span, HEAD)
+        values = kv_ref[m, at, :, HEAD:].reshape(span, HEAD)
+        keys_t = keys.T
+        key_total = jnp.zeros((span, HEAD), F32)
+        value_total = jnp.zeros((span, HEAD), F32)
+        for pair in range(heads // 2):
+            band = slice(pair * 2 * micro, (pair + 1) * 2 * micro)
+            probs = probs_ref[hm, :, band]
+            grads = grad_mixed[hm, band, :]
+            queries = qs_ref[hm, band, :]
+            value_total = value_total + mm(probs, grads)
+            grad_probs = mm_nt(values, grads)
+            wide = probs.astype(F32)
+            delta = jnp.sum(grad_probs * wide, axis=0, keepdims=True)
+            grad_scores = (wide * (grad_probs - delta)).astype(BF16)
+            key_total = key_total + mm(grad_scores, queries)
+            query_t = mm(keys_t, grad_scores) * score_scale
+            for i in range(2):
+                head = pair * 2 + i
+                one = query_t[:, i * micro : (i + 1) * micro].T
+                grad_q[hm, :, head * HEAD : (head + 1) * HEAD] = turned(
+                    one, cos_ref[hm], -sin_ref[hm]
+                ).astype(BF16)
+        key_total = (key_total * score_scale).reshape(2 * reach + 1, micro, HEAD)
+        kv_total[m, at, :, 0:HEAD] = kv_total[m, at, :, 0:HEAD] + key_total
+        kv_total[m, at, :, HEAD:] = kv_total[m, at, :, HEAD:] + value_total.reshape(
+            2 * reach + 1, micro, HEAD
+        )
+        return carry
+
+    lax.fori_loop(0, 4, attend_back, 0)
+
+    kv_give[...] = kv_total[...].astype(BF16)
+
+    def kv_copy(j, core):
+        return pltpu.make_async_remote_copy(
+            src_ref=kv_give.at[:, 2 * reach - 2 * j + core],
+            dst_ref=kv_got.at[2 * j + f],
+            send_sem=kv_send.at[j, core],
+            recv_sem=kv_recv.at[2 * j + f],
+            device_id=(d - j, core),
+            device_id_type=MESH,
+        )
+
+    sent.remote(
+        kv_give.at[:, 2 * reach + other],
+        kv_got.at[f],
+        kv_send.at[0, 0],
+        kv_recv.at[f],
+        (d, other),
+    )
+    for j in range(1, reach + 1):
+
+        @pl.when(d - j >= 0)
+        def _():
+            for core in range(2):
+                kv_copy(j, core).start()
+
+    lows_t[:, 0:rows] = low_ref[0].T
+    lows_t[:, rows:] = low_ref[1].T
+    tile = 2 * HEAD
+    for hm in range(4):
+        mixed_rows[hm * micro : (hm + 1) * micro, :] = mixed_ref[hm]
+
+    def out_tile(i, carry):
+        at = pl.ds(pl.multiple_of(i * tile, tile), tile)
+        got_ref[at, :] = mm(lows_t[at, :], mixed_rows[...]).astype(BF16)
+        return carry
+
+    lax.fori_loop(0, width // tile, out_tile, 0)
+    lows_t[:, 0:rows] = n1_ref[0].T
+    lows_t[:, rows:] = n1_ref[1].T
+    for hm in range(4):
+        mixed_rows[hm * micro : (hm + 1) * micro, :] = grad_q[hm]
+
+    def query_tile(i, carry):
+        at = pl.ds(pl.multiple_of(i * tile, tile), tile)
+        gq_ref[at, :] = mm(lows_t[at, :], mixed_rows[...]).astype(BF16)
+        return carry
+
+    lax.fori_loop(0, width // tile, query_tile, 0)
+
+    def one_back(h):
+        band = pl.ds(pl.multiple_of(h * rows, rows), rows)
+        return mm_nt(mixed_rows[band, :], wq_ref[...])
+
+    one_out[...] = one_back(other).astype(BF16)
+    sent.remote(one_out, one_in, one_sems.at[0], one_sems.at[1], (d, other))
+    grad_one = one_back(f)
+
+    sums = [kv_total[m, 2 * reach + f] for m in range(MICRO)]
+    arrived(kv_got.at[other], kv_recv.at[other])
+    sums = [sums[m] + kv_got[other, m].astype(F32) for m in range(MICRO)]
+    for j in range(1, reach + 1):
+        for core in range(2):
+            slot = 2 * j + core
+
+            @pl.when(d + j < chips)
+            def _():
+                arrived(kv_got.at[slot], kv_recv.at[slot])
+
+            @pl.when(d + j >= chips)
+            def _():
+                kv_got[slot] = jnp.zeros((MICRO, micro, 2 * HEAD), BF16)
+
+            sums = [sums[m] + kv_got[slot, m].astype(F32) for m in range(MICRO)]
+    key_rows = jnp.concatenate(
+        [
+            turned(sums[m][:, 0:HEAD], cos_ref[2 * f + m], -sin_ref[2 * f + m])
+            for m in range(MICRO)
+        ],
+        axis=0,
+    )
+    value_rows = jnp.concatenate([sums[m][:, HEAD:] for m in range(MICRO)], axis=0)
+    pieces = halves_in(key_rows, value_rows)
+    n1_own_t = n1_ref[f].T
+    row_values = rows_ref[...].astype(F32)
+    for i in range(2):
+        piece = pieces[i].astype(BF16)
+        gkvg_ref[i, :, 0:share, :] = (
+            mm(n1_own_t, piece).astype(BF16).reshape(chips, share, HEAD)
+        )
+        grad_one = grad_one + mm_nt(piece, kvg_ref[i, :, 0:share, :].reshape(width, HEAD))
+    arrived(one_in, one_sems.at[1])
+    grad_one = grad_one + one_in[...].astype(F32)
+    gain_one = gain_row(kvg_ref, 0, chips, width, share)
+    back_one, gain_one_grad = norm_back(row_values, gain_one, grad_one)
+    grad_rows_ref[...] = (grad_middle + back_one).astype(BF16)
+    spread = gain_spread(width, share)
+    stretch = own_stretch(chips, width, share)
+    for i, grad in enumerate((gain_one_grad, gain_two_grad)):
+        piece = mm_nt(jnp.where(stretch, grad, 0.0).astype(BF16), spread)
+        row = iota((chips, 16, HEAD), 1)
+        gkvg_ref[i, :, share : share + 16, :] = jnp.where(
+            row == 0, piece[:, None, :], 0.0
+        ).astype(BF16)
+
+    for j in range(1, reach + 1):
+
+        @pl.when(d - j >= 0)
+        def _():
+            for core in range(2):
+                kv_copy(j, core).wait_send()
+
+    sent.finish()
+
+
+def attention_back(chips, reach, rows_in, pg, middle, two, n1, qs, kv, probs, mixed, wq, wot, kvg, cosine, sine):
+    rows, width = rows_in.shape
+    micro = rows // MICRO
+    heads = wq.shape[1] // HEAD
+    slots = 2 * reach + 2
+    dma = pltpu.SemaphoreType.DMA
+    shape = jax.ShapeDtypeStruct
+    return pl.pallas_call(
+        functools.partial(attention_back_kernel, chips, reach),
+        out_shape=(
+            shape((rows, width), BF16),
+            shape(wq.shape, BF16),
+            shape(wot.shape, BF16),
+            shape(kvg.shape, BF16),
+        ),
+        in_specs=[VM] * 14,
+        out_specs=(VM,) * 4,
+        scratch_shapes=[
+            pltpu.VMEM((2, rows, width), BF16),
+            pltpu.VMEM((width, 2 * rows), BF16),
+            pltpu.VMEM((2 * rows, heads * HEAD), BF16),
+            pltpu.VMEM((4, heads * micro, HEAD), BF16),
+            pltpu.VMEM((4, micro, heads * HEAD), BF16),
+            pltpu.VMEM((MICRO, slots, micro, 2 * HEAD), F32),
+            pltpu.VMEM((MICRO, slots, micro, 2 * HEAD), BF16),
+            pltpu.VMEM((slots, MICRO, micro, 2 * HEAD), BF16),
+            pltpu.VMEM((rows, width), BF16),
+            pltpu.VMEM((rows, width), BF16),
+            dma((2,)),
+            dma((reach + 1, 2)),
+            dma((slots,)),
+            dma((2,)),
+        ],
+        compiler_params=pltpu.CompilerParams(
+            collective_id=3, has_side_effects=True, vmem_limit_bytes=VMEM_ASK
+        ),
+        name="attention_backward",
+    )(rows_in, pg, middle, two, n1, qs, kv, probs, mixed, wq, wot, kvg, cosine, sine)
+
+
+def scatter_kernel(
+    chips,
+    three_ref,
+    gq_ref,
+    got_ref,
+    gkvg_ref,
+    outs_ref,
+    grad_rows_ref,
+    take_ref,
+    place_ref,
+    three_out,
+    q_out,
+    ot_out,
+    kvg_out,
+    output_ref,
+    input_grad_ref,
+    pair_got,
+    three_give,
+    three_got,
+    kvg_got,
+    attn_got,
+    attn_give,
+    attn_last,
+    kvg_fan,
+    kvg_give,
+    kvg_last,
+    give,
+    got,
+    pair_send,
+    pair_recv,
+    three_send,
+    three_recv,
+    kvg_sems,
+    fan_send,
+    fan_recv,
+    column_send,
+    column_recv,
+    row_send,
+    row_recv,
+):
+    place = Place(chips)
+    d, f, other = place.d, place.f, place.other
+    groups = place.groups
+    rows, width = outs_ref.shape
+    share = width // chips
+    half = share // 2
+    part = three_ref.shape[2]
+    per = rows // chips
+    sent = Sent()
+    greet_all(place)
+
+    def order(k, j):
+        return ((place.g + k) % groups) * PLANE + place.plane_pos(j)
+
+    def band(s, core):
+        return pl.ds(pl.multiple_of(s * share + half * core, 16), half)
+
+    steps = [(k, j) for k in range(groups) for j in range(PLANE)]
+    steps = steps[1:] + steps[:1]
+    sent.remote(gkvg_ref.at[other], kvg_got, kvg_sems.at[0], kvg_sems.at[1], (d, other))
+    for k, j in steps:
+        s = order(k, j)
+        sent.remote(
+            three_ref.at[:, band(s, other)],
+            pair_got.at[s],
+            pair_send.at[s],
+            pair_recv.at[s],
+            (d, other),
+        )
+
+    def whole(s):
+        return pl.ds(pl.multiple_of(s * share, 16), share)
+
+    attn = (gq_ref, got_ref)
+    for j in range(1, PLANE):
+        to = place.plane_pos(j)
+        for k in range(groups):
+            s = ((place.g + k) % groups) * PLANE + to
+            for a in range(2):
+                sent.remote(
+                    attn[a].at[whole(s)],
+                    attn_got.at[a, j, s // PLANE],
+                    fan_send.at[a, j, k],
+                    fan_recv.at[a, j, s // PLANE],
+                    (place.plane_chip(j), f),
+                )
+
+    def block(k):
+        return pl.ds(pl.multiple_of(k * per, per), per)
+
+    give[:, :width] = mm_tn(place_ref[...], outs_ref[...]).astype(BF16)
+    give[:, width:] = mm_tn(place_ref[...], grad_rows_ref[...]).astype(BF16)
+    for k in range(1, chips):
+        to = (d + k) % chips
+        sent.remote(give.at[block(to)], got.at[block(d)], row_send.at[k], row_recv.at[d], (to, f))
+    got[block(d), :] = give[block(d), :]
+
+    arrived(kvg_got, kvg_sems.at[1])
+    for s in range(chips):
+        kvg_give[s] = (gkvg_ref[f, s].astype(F32) + kvg_got[s].astype(F32)).astype(BF16)
+    for j in range(1, PLANE):
+        to = place.plane_pos(j)
+        for k in range(groups):
+            s = ((place.g + k) % groups) * PLANE + to
+            sent.remote(
+                kvg_give.at[s],
+                kvg_fan.at[j, s // PLANE],
+                fan_send.at[2, j, k],
+                fan_recv.at[2, j, s // PLANE],
+                (place.plane_chip(j), f),
+            )
+
+    def three_slot(j_x, k):
+        return 2 * k + j_x
+
+    for n, (k, j) in enumerate(steps):
+        s = order(k, j)
+        arrived(pair_got.at[s], pair_recv.at[s])
+        for a in range(3):
+            three_give[s, a] = (
+                three_ref[a, band(s, f), :].astype(F32) + pair_got[s, a].astype(F32)
+            ).astype(BF16)
+        dst = three_got.at[2 * place.g + place.x, f]
+        recv = three_recv.at[2 * place.g + place.x, f]
+        if (k, j) == (0, 0):
+            remote = pltpu.make_async_remote_copy(
+                src_ref=three_give.at[s],
+                dst_ref=dst,
+                send_sem=three_send.at[s],
+                recv_sem=recv,
+                device_id=(d, other),
+                device_id_type=MESH,
+            )
+
+            @pl.when(place.y != f)
+            def _():
+                remote.start()
+
+            @pl.when(place.y == f)
+            def _():
+                three_got[2 * place.g + place.x, f] = three_give[s]
+
+            own_remote = remote
+        else:
+            sent.remote(three_give.at[s], dst, three_send.at[s], recv, (s, place.y))
+
+    for k in list(range(1, groups)) + [0]:
+        g = (place.g + k) % groups
+        s = g * PLANE + place.p
+        for a in range(2):
+            total = attn[a][whole(s), :].astype(F32)
+            for j in range(1, PLANE):
+                arrived(attn_got.at[a, j, g], fan_recv.at[a, j, g])
+                total = total + attn_got[a, j, g].astype(F32)
+            if k == 0:
+                (q_out, ot_out)[a][...] = total
+            else:
+                attn_give[a, g] = total.astype(BF16)
+                sent.remote(
+                    attn_give.at[a, g],
+                    attn_last.at[a, place.g],
+                    column_send.at[a, k],
+                    column_recv.at[a, place.g],
+                    (s, f),
+                )
+        total = kvg_give[s].astype(F32)
+        for j in range(1, PLANE):
+            arrived(kvg_fan.at[j, g], fan_recv.at[2, j, g])
+            total = total + kvg_fan[j, g].astype(F32)
+        if k == 0:
+            kvg_out[...] = total
+        else:
+            kvg_give[s] = total.astype(BF16)
+            sent.remote(
+                kvg_give.at[s],
+                kvg_last.at[place.g],
+                column_send.at[2, k],
+                column_recv.at[2, place.g],
+                (s, f),
+            )
+
+    for k in range(1, chips):
+        s = (d + k) % chips
+        arrived(got.at[block(s)], row_recv.at[s])
+    output_ref[...] = mm_tn(take_ref[...], got[:, :width]).astype(BF16)
+    input_grad_ref[...] = mm_tn(take_ref[...], got[:, width:]).astype(BF16)
+
+    for k in range(1, groups):
+        g = (place.g + k) % groups
+        for a in range(2):
+            arrived(attn_last.at[a, g], column_recv.at[a, g])
+            out = (q_out, ot_out)[a]
+            out[...] = out[...] + attn_last[a, g].astype(F32)
+        arrived(kvg_last.at[g], column_recv.at[2, g])
+        kvg_out[...] = kvg_out[...] + kvg_last[g].astype(F32)
+
+    for cx in range(2):
+        for core in range(2):
+            for k in range(groups):
+                g = (place.g + k) % groups
+                slot = 2 * g + cx
+                piece = three_got.at[slot, core]
+
+                if k == 0:
+                    @pl.when((place.y != f) | (place.x != cx) | (core != f))
+                    def _():
+                        arrived(piece, three_recv.at[slot, core])
+                else:
+                    arrived(piece, three_recv.at[slot, core])
+            for a in range(3):
+                total = three_got[cx, core, a].astype(F32)
+                for g in range(1, groups):
+                    total = total + three_got[2 * g + cx, core, a].astype(F32)
+                three_out[a, half * core : half * (core + 1), cx * part : (cx + 1) * part] = total
+
+    @pl.when(place.y != f)
+    def _():
+        own_remote.wait_send()
+
+    sent.finish()
+
+
+def scatter(chips, three, gq, got, gkvg, outs, grad_rows, take, placing):
+    rows, width = outs.shape
+    share = width // chips
+    half = share // 2
+    part = three.shape[2]
+    groups = chips // PLANE
+    heads_wide = gq.shape[1]
+    small = gkvg.shape[2:]
+    dma = pltpu.SemaphoreType.DMA
+    shape = jax.ShapeDtypeStruct
+    return pl.pallas_call(
+        functools.partial(scatter_kernel, chips),
+        out_shape=(
+            shape((3, share, 2 * part), F32),
+            shape((share, heads_wide), F32),
+            shape((share, heads_wide), F32),
+            shape(small, F32),
+            shape((rows, width), BF16),
+            shape((rows, width), BF16),
+        ),
+        in_specs=[VM] * 8,
+        out_specs=(VM,) * 6,
+        scratch_shapes=[
+            pltpu.VMEM((chips, 3, half, part), BF16),
+            pltpu.VMEM((chips, 3, half, part), BF16),
+            pltpu.VMEM((2 * groups, 2, 3, half, part), BF16),
+            pltpu.VMEM((chips,) + small, BF16),
+            pltpu.VMEM((2, PLANE, groups, share, heads_wide), BF16),
+            pltpu.VMEM((2, groups, share, heads_wide), BF16),
+            pltpu.VMEM((2, groups, share, heads_wide), BF16),
+            pltpu.VMEM((PLANE, groups) + small, BF16),
+            pltpu.VMEM((chips,) + small, BF16),
+            pltpu.VMEM((groups,) + small, BF16),
+            pltpu.VMEM((rows, 2 * width), BF16),
+            pltpu.VMEM((rows, 2 * width), BF16),
+            dma((chips,)),
+            dma((chips,)),
+            dma((chips,)),
+            dma((2 * groups, 2)),
+            dma((2,)),
+            dma((3, PLANE, groups)),
+            dma((3, PLANE, groups)),
+            dma((3, groups)),
+            dma((3, groups)),
+            dma((chips,)),
+            dma((chips,)),
+        ],
+        compiler_params=pltpu.CompilerParams(
+            collective_id=4, has_side_effects=True, vmem_limit_bytes=VMEM_ASK
+        ),
+        name="scatter_grads_and_rows",
+    )(three, gq, got, gkvg, outs, grad_rows, take, placing)
+
+
+def planned(
+    tokens,
+    cotangent,
+    deal,
+    first_len,
+    w_query,
+    w_key,
+    w_value,
+    w_out,
+    w_gate,
+    w_up,
+    w_down,
+    norm_gains,
+):
+    chips = lax.axis_size("dp")
+    rows, width = tokens.shape
+    micro = rows // MICRO
+    share = w_query.shape[0]
+    back_blocks = min(2 * chips - 1, (WINDOW + micro - 2) // micro)
+    reach = (back_blocks + 1) // 2
+    d = lax.axis_index("dp")
+    inside = jnp.arange(micro, dtype=jnp.int32)
+    positions = (2 * d + jnp.arange(2, dtype=jnp.int32))[:, None, None] * micro + inside
+    second = positions >= first_len[None, :, None]
+    within = positions - jnp.where(second, first_len[None, :, None], 0)
+    cosine, sine = angles(within.reshape(-1))
+    cosine = jnp.concatenate([cosine, cosine], axis=1).reshape(4, micro, HEAD)
+    sine = jnp.concatenate([-sine, sine], axis=1).reshape(4, micro, HEAD)
+    gain_rows = jnp.pad(norm_gains, ((0, 15), (0, HEAD - share)))
+    kvg = jnp.concatenate([jnp.concatenate([w_key, w_value], axis=1), gain_rows], axis=0)
+    wq, wot, kvg_all, three, rows_in, pg_all, take, placing = gather(
+        chips, deal, tokens, cotangent, w_query, w_out.T, kvg, w_gate, w_up, w_down.T
+    )
+    n1, qs, kv, probs, mixed, middle, n2 = attention(
+        chips, reach, first_len, rows_in, wq, wot, kvg_all, cosine, sine
+    )
+    outs, grad_two, three_grads = mlp(chips, n2, middle, pg_all, three)
+    pg = lax.dynamic_index_in_dim(pg_all, d % PLANE, 0, keepdims=False)
+    grad_rows, gq, got, gkvg = attention_back(
+        chips, reach, rows_in, pg, middle, grad_two, n1, qs, kv, probs, mixed, wq, wot, kvg_all,
+        cosine, sine,
+    )
+    three_out, q_out, ot_out, kvg_out, output, input_grad = scatter(
+        chips, three_grads, gq, got, gkvg, outs, grad_rows, take, placing
+    )
+    key_cols = w_key.shape[1]
+    return (
+        output,
+        input_grad,
+        q_out,
+        kvg_out[:share, :key_cols],
+        kvg_out[:share, key_cols:],
+        ot_out.T,
+        three_out[0],
+        three_out[1],
+        three_out[2].T,
+        kvg_out[share : share + 1, :share],
+    )
+
+
+def fits_plan(mesh, share):
+    chips = mesh.shape["dp"]
+    return mesh.shape["fsdp"] == 2 and chips % PLANE == 0 and share % 32 == 0 and share < HEAD
+
+
 def solution(mesh):
     in_specs = (
         P(("dp", "fsdp"), None),
@@ -393,6 +1807,11 @@
         P("fsdp", "dp"),
         P("fsdp", "dp"),
     )
-    return jax.shard_map(
-        per_device, mesh=mesh, in_specs=in_specs, out_specs=out_specs, check_vma=False
-    )
+    def placed(*arrays):
+        share = arrays[4].shape[0] // mesh.shape["dp"]
+        program = planned if fits_plan(mesh, share) else per_device
+        return jax.shard_map(
+            program, mesh=mesh, in_specs=in_specs, out_specs=out_specs, check_vma=False
+        )(*arrays)
+
+    return placed

time: 2420 us -> 699 us (0.29)
  waiting for transfers between devices: 1660 us -> 0 us
  Pallas kernels: 0 us -> 676 us
  matrix products: 259 us -> 0 us
  blocking collectives: 145 us -> 0 us
  starting transfers between devices: 131 us -> 0 us
  local copies, waits for them, and re-layouts: 131 us -> 13.7 us
  other arithmetic: 64.7 us -> 2.85 us
    unnamed x30 -> x0, waiting for transfers between devices: 690 us -> none
    pallas_call x0 -> x5, Pallas kernels: none -> 676 us  [the longest x1 229 us: gather(): pl.pallas_call(functools.partial(gather_kernel, chips), out_shape=(jax.Sh...]
    reduce_scatter x10 -> x0, waiting for transfers between devices: 620 us -> none  [the longest x1 228 us: per_device(): lax.psum_scatter(sectioned[5], 'dp', scatter_dimension=0, tiled=True)]
    all_gather x10 -> x0, waiting for transfers between devices: 330 us -> none  [the longest x1 102 us: per_device(): lax.all_gather(w_gate, 'dp', axis=0, tiled=True)]
    dot_general x105 -> x0, matrix products: 259 us -> none  [the longest x7 52.8 us: against(): lax.dot_general(left, right, (((1,), (1,)), ((), ())), preferred_element_...]
    ppermute x32 -> x0, starting transfers between devices: 87.5 us -> none  [passed_along(): return lax.ppermute(x, axis, pairs)]
    all_gather x5 -> x0, blocking collectives: 83 us -> none  [the longest x1 42.4 us: per_device(): lax.all_gather(w_key, 'dp', axis=0, tiled=True)]
    unnamed x2 -> x0, blocking collectives: 62.1 us -> none
  transfers between devices with their start and end apart: 62 -> 0, of which waited for: 20 -> 0; matrix products, arithmetic and copies ran while one was open for 10% -> 0% of each run, Pallas kernels for 0% -> 0%
where the time goes in v1:
time: 699 us; the launch traced here: 694 us
  Pallas kernels  676 us (97%)
  local copies, waits for them, and re-layouts  13.7 us (2%)
    pallas_call x1, Pallas kernels, gather(): pl.pallas_call(functools.partial(gather_kernel, chips), out_shape=(jax.Sh...  229 us
    pallas_call x1, Pallas kernels, scatter(): pl.pallas_call(functools.partial(scatter_kernel, chips), out_shape=(shape...  217 us
    pallas_call x1, Pallas kernels, mlp(): pl.pallas_call(functools.partial(mlp_kernel, chips), out_shape=(shape((ro...  126 us
    pallas_call x1, Pallas kernels, attention_back(): pl.pallas_call(functools.partial(attention_back_kernel, chips, reach), ou...  54.6 us
    pallas_call x1, Pallas kernels, attention(): pl.pallas_call(functools.partial(attention_kernel, chips, reach), out_sha...  48.9 us

profile of v1, /device:TPU:26, one launch (start us, length us, event | category | flops | bytes accessed | tf_op | source)
XLA Modules:
  0.0 693.6 jit_solution(2039093579265325826)
XLA Ops:
  0.6 0.0 copy-start.7
  0.7 0.0 copy-start.5
  0.7 0.0 copy-start.6
  0.7 0.0 copy-start.8
  0.7 0.1 iota_add_fusion
  0.8 0.7 ge.20
  1.4 0.1 ge.21
  1.5 0.1 subtract_convert_fusion
  1.6 1.0 fusion
  2.6 1.0 pad_maximum_fusion
  3.6 1.5 broadcast_in_dim.15.deal_col_ref
  5.1 0.0 copy-done.5
  5.1 0.1 copy.22
  5.2 0.0 copy-done.6
  5.2 0.1 copy.23
  5.3 0.0 copy-done.8
  5.3 0.7 fusion.2.kvg_ref
  6.0 0.0 copy-done.7
  6.0 0.6 broadcast_in_dim.14.deal_ref
  6.6 229.3 %gather_weights_and_rows.1 = (bf16[1536,768]{1,0:T(8,128)(2,1)}, bf16[1536,768]{1,0:T(8,128)(2,1)}, bf16[2,16,112,128]{3,2,1,0:T(8,128)(2,1)}, bf16[3,1536,1152]...) custom-call(s32[8,256]{1,0:T(8,128)} %broadcast_in_dim.14.deal_ref, ...), custom_call_target="tpu_custom_call" | custom-call | tf_op jit(solution)/shard_map/gather_weights_and_rows/pallas_call | solution.py:739
  235.9 48.9 %attention_forward.1 = (bf16[2,256,1536]{2,1,0:T(8,128)(2,1)}, bf16[4,768,128]{2,1,0:T(8,128)(2,1)}, bf16[2,10,128,256]{3,2,1,0:T(8,128)(2,1)}, bf16[4,1152,768]...) custom-call(s32[2]{0:T(128)} %first_ref.1, ...), custom_call_target="tpu_custom_call" | custom-call | tf_op jit(solution)/shard_map/attention_forward/pallas_call | solution.py:967
  284.8 125.9 %mlp_both_ways.1 = (bf16[256,1536]{1,0:T(8,128)(2,1)}, f32[256,1536]{1,0:T(8,128)}, bf16[3,1536,1152]{2,1,0:T(8,128)(2,1)}) custom-call(bf16[256,1536]{1,0:T(8,128)(2,1)} %get-tuple-element.42.n2_ref, f32[256,1536]{1,0:T(8,128)} %get-tuple-element.43.middle_ref, bf16[4,256,1536]{2,1,0:T(8,128)(2,1)} %get-tuple-element.44.pg_ref, ...), custom_call_target="tpu_custom_call" | custom-call | tf_op jit(solution)/shard_map/mlp_both_ways/pallas_call | solution.py:1150
  410.7 2.1 dynamic-slice_bitcast_fusion.pg_ref
  412.8 54.6 %attention_backward.1 = (bf16[256,1536]{1,0:T(8,128)(2,1)}, bf16[1536,768]{1,0:T(8,128)(2,1)}, bf16[1536,768]{1,0:T(8,128)(2,1)}, bf16[2,16,112,128]{3,2,1,0:T(8,128)(2,1)}) custom-call(bf16[256,1536]{1,0:T(8,128)(2,1)} %get-tuple-element.38.rows_ref, bf16[256,1536]{1,0:T(8,128)(2,1)} %dynamic-slice_bitcast_fusion.pg_ref, ...), custom_call_target="tpu_custom_call" | custom-call | tf_op jit(solution)/shard_map/attention_backward/pallas_call | solution.py:1409
  467.4 217.1 %scatter_grads_and_rows.1 = (f32[3,96,2304]{2,1,0:T(8,128)}, f32[96,768]{1,0:T(8,128)}, f32[96,768]{1,0:T(8,128)}, f32[112,128]{1,0:T(8,128)}, bf16[256,1536]{1,0:T(8,128)(2,1)}, /*index=5*/bf16[256,1536]{1,0:T(8,128)(2,1)}) custom-call(bf16[3,1536,1152]{2,1,0:T(8,128)(2,1)} %get-tuple-element.46.three_ref, bf16[1536,768]{1,0:T(8,128)(2,1)} %get-tuple-element.53.gq_ref, ...), custom_call_target="tpu_custom_call" | custom-call | tf_op jit(solution)/shard_map/scatter_grads_and_rows/pallas_call | solution.py:1674
  684.5 0.0 copy-start.4
  684.5 0.0 copy-start.1
  684.6 0.0 copy-start
  684.6 3.4 slice_bitcast_fusion
  687.9 0.0 copy-start.3
  687.9 0.0 copy-start.2
  687.9 0.0 copy-done.4
  687.9 0.1 fusion.3
  688.0 0.7 copy.24
  688.7 0.7 copy.25
  689.4 0.5 slice.23
  689.9 0.0 copy-done.1
  689.9 0.9 copy.30
  690.8 0.0 copy-done
  690.8 0.9 copy.31
  691.7 0.0 copy-done.3
  691.7 0.7 copy.32
  692.4 0.0 copy-done.2
  692.4 0.7 copy.33
  (3 shorter events, 0.0 us)
Async XLA Ops:
  0.6 5.4 copy-start.7
  0.7 4.4 copy-start.5
  0.7 4.5 copy-start.6
  0.7 4.6 copy-start.8
  684.5 3.4 copy-start.4
  684.5 5.4 copy-start.1
  684.6 6.3 copy-start
  687.9 3.8 copy-start.3
  687.9 4.5 copy-start.2

commit v2 on v1

--- a/solution.py
+++ b/solution.py
@@ -477,10 +477,100 @@
     return jnp.sum(jnp.where(own_stretch(chips, width, share), spread, 0.0), axis=0, keepdims=True)
 
 
-def gather_kernel(
+def rms_scale(values):
+    return lax.rsqrt(jnp.mean(values * values, axis=-1, keepdims=True) + EPSILON)
+
+
+def turned(values, cosine, sine):
+    return values * cosine + pltpu.roll(values, HEAD // 2, 1) * sine
+
+
+def halves_in(first, second):
+    front = iota(first.shape, 1) < HEAD // 2
+    return (
+        jnp.where(front, first, pltpu.roll(second, HEAD // 2, 1)),
+        jnp.where(front, pltpu.roll(first, HEAD // 2, 1), second),
+    )
+
+
+class Chain:
+    def __init__(self, place, piece, count, up_sems, down_sems, recv_sems):
+        self.place, self.piece, self.count = place, piece, count
+        self.up_sems, self.down_sems, self.recv_sems = up_sems, down_sems, recv_sems
+        self.has_up = place.g + 1 < place.groups
+        self.has_down = place.g >= 1
+
+    def hop(self, a, origin, up):
+        place = self.place
+        ref = self.piece(a, origin)
+        to = place.d + PLANE if up else place.d - PLANE
+        sems = self.up_sems if up else self.down_sems
+        return pltpu.make_async_remote_copy(
+            src_ref=ref,
+            dst_ref=ref,
+            send_sem=sems.at[a, origin],
+            recv_sem=self.recv_sems.at[a, origin],
+            device_id=(to, place.f),
+            device_id_type=MESH,
+        )
+
+    def start(self, a):
+        def one(up):
+            self.hop(a, self.place.g, up).start()
+
+        pl.when(self.has_up)(functools.partial(one, True))
+        pl.when(self.has_down)(functools.partial(one, False))
+
+    def step(self, k, arrays, then):
+        place = self.place
+
+        def from_below():
+            origin = place.g - k
+            for a in arrays:
+                arrived(self.piece(a, origin), self.recv_sems.at[a, origin])
+
+                @pl.when(self.has_up)
+                def _():
+                    self.hop(a, origin, True).start()
+
+                then(a, origin)
+
+        def from_above():
+            origin = place.g + k
+            for a in arrays:
+                arrived(self.piece(a, origin), self.recv_sems.at[a, origin])
+
+                @pl.when(self.has_down)
+                def _():
+                    self.hop(a, origin, False).start()
+
+                then(a, origin)
+
+        pl.when(place.g >= k)(from_below)
+        pl.when(place.g + k < place.groups)(from_above)
+
+    def finish(self):
+        place = self.place
+        for k in range(place.groups):
+            for a in range(self.count):
+
+                @pl.when((place.g >= k) & self.has_up)
+                def _():
+                    self.hop(a, place.g - k, True).wait_send()
+
+                @pl.when((place.g + k < place.groups) & self.has_down)
+                def _():
+                    self.hop(a, place.g + k, False).wait_send()
+
+
+def forward_kernel(
     chips,
+    reach,
+    first_ref,
     deal_ref,
     deal_col_ref,
+    cos_ref,
+    sin_ref,
     tokens_ref,
     cot_ref,
     wq_ref,
@@ -489,140 +579,190 @@
     gate_ref,
     up_ref,
     down_ref,
+    full_three,
     full_q,
     full_ot,
     full_kvg,
-    full_three,
     rows_out,
     pg_all,
     take_ref,
     place_ref,
+    n1_ref,
+    qs_ref,
+    kv_ref,
+    probs_ref,
+    mixed_ref,
+    middle_ref,
+    n2_all,
     deal_all,
     give,
     got,
+    bias_ref,
+    branch_out,
+    branch_in,
     deal_send,
     deal_recv,
     row_send,
     row_recv,
-    attn_send,
+    attn_up,
+    attn_down,
     attn_recv,
     fan_send,
-    kv_sems,
-    three_send,
+    fan_recv,
+    kvg_sems,
+    stage_send,
+    stage_recv,
+    three_up,
+    three_down,
     three_recv,
     relay_send,
     relay_recv,
-    own_sems,
-    pg_send,
-    pg_recv,
+    plane_send,
+    plane_recv,
+    n1_sems,
+    kv_send,
+    kv_recv,
+    branch_sems,
     local_sems,
 ):
     place = Place(chips)
     d, f, other = place.d, place.f, place.other
+    groups = place.groups
     rows, width = tokens_ref.shape
     share = wq_ref.shape[0]
     half = share // 2
     per = rows // chips
     part = gate_ref.shape[1] // 2
+    micro = rows // MICRO
+    heads = wq_ref.shape[1] // HEAD
+    span = (2 * reach + 1) * micro
     sent = Sent()
     greet_all(place)
 
     deal_all[d] = deal_ref[...]
     for k in range(1, chips):
         to = (d + k) % chips
-        sent.remote(
-            deal_all.at[d], deal_all.at[d], deal_send.at[k], deal_recv.at[d], (to, f)
-        )
-
-    def attn_slices(s):
+        sent.remote(deal_all.at[d], deal_all.at[d], deal_send.at[k], deal_recv.at[d], (to, f))
+
+    def attn_piece(a, s):
+        if a == 0:
+            return full_kvg.at[f, s]
         band = pl.ds(pl.multiple_of(s * share, 16), share)
-        return (full_q.at[band], full_ot.at[band], full_kvg.at[f, s])
-
-    mine = attn_slices(d)
-    sources = (wq_ref, wot_ref, kvg_ref)
+        return (full_q if a == 1 else full_ot).at[band]
+
+    own_attn = (kvg_ref, wq_ref, wot_ref)
+    copies = [
+        pltpu.make_async_copy(own_attn[a], attn_piece(a, d), local_sems.at[a]) for a in range(3)
+    ]
+    for copy in copies:
+        copy.start()
+    for copy in copies:
+        copy.wait()
+    attn = Chain(
+        place, lambda a, g: attn_piece(a, g * PLANE + place.p), 3, attn_up, attn_down, attn_recv
+    )
+
+    def fan(a, g):
+        for j in range(1, PLANE if a == 0 else PLANE - 1):
+            fan_copy(a, g, j).start()
+
+    def fan_copy(a, g, j):
+        s = g * PLANE + place.p
+        return pltpu.make_async_remote_copy(
+            src_ref=attn_piece(a, s),
+            dst_ref=attn_piece(a, s),
+            send_sem=fan_send.at[a, g, j],
+            recv_sem=fan_recv.at[a, s],
+            device_id=(place.plane_chip(j), f),
+            device_id_type=MESH,
+        )
+
+    def pass_copy(a, g):
+        by_x = place.plane_pos(1)
+        by_y = place.plane_pos(2)
+        even = g % 2 == 0
+        s = g * PLANE + jnp.where(even, by_x, by_y)
+        to = jnp.where(even, place.plane_chip(2), place.plane_chip(1))
+        return pltpu.make_async_remote_copy(
+            src_ref=attn_piece(a, s),
+            dst_ref=attn_piece(a, s),
+            send_sem=fan_send.at[a, g, PLANE - 1],
+            recv_sem=fan_recv.at[a, s],
+            device_id=(to, f),
+            device_id_type=MESH,
+        )
+
+    def pass_on(a, g):
+        s = g * PLANE + jnp.where(g % 2 == 0, place.plane_pos(1), place.plane_pos(2))
+        arrived(attn_piece(a, s), fan_recv.at[a, s])
+        pass_copy(a, g).start()
+
+    def pass_all(a):
+        pass_on(a, place.g)
+        for k in range(1, groups):
+            pl.when(place.g >= k)(functools.partial(pass_on, a, place.g - k))
+            pl.when(place.g + k < groups)(functools.partial(pass_on, a, place.g + k))
+
+    for a in range(2):
+        attn.start(a)
+        fan(a, place.g)
+    attn.start(2)
+
+    mats = (gate_ref, up_ref, down_ref)
+
+    def stage_src(a, to_x, core):
+        return mats[a].at[pl.ds(half * core, half), pl.ds(pl.multiple_of(part * to_x, 128), part)]
+
+    def stage_copy(a, b, core):
+        to_x = (place.x + b) % 2
+        return pltpu.make_async_remote_copy(
+            src_ref=stage_src(a, to_x, core),
+            dst_ref=full_three.at[a, d, core],
+            send_sem=stage_send.at[a, b, core],
+            recv_sem=stage_recv.at[a, place.p],
+            device_id=(place.g * PLANE + 2 * f + to_x, core),
+            device_id_type=MESH,
+        )
+
+    def own_copy(a):
+        return pltpu.make_async_copy(
+            mats[a].at[pl.ds(pl.multiple_of(half * f, 16), half), pl.ds(pl.multiple_of(part * place.x, 128), part)],
+            full_three.at[a, d, f],
+            local_sems.at[a],
+        )
+
+    def pair_copy(a):
+        return pltpu.make_async_remote_copy(
+            src_ref=mats[a].at[
+                pl.ds(pl.multiple_of(half * other, 16), half),
+                pl.ds(pl.multiple_of(part * place.x, 128), part),
+            ],
+            dst_ref=full_three.at[a, d, other],
+            send_sem=stage_send.at[a, 0, 0],
+            recv_sem=stage_recv.at[a, place.p],
+            device_id=(d, other),
+            device_id_type=MESH,
+        )
+
     for a in range(3):
-        for k in range(1, place.groups):
-            sent.remote(
-                sources[a], mine[a], attn_send.at[a, k], attn_recv.at[a, d], (place.column_chip(k), f)
-            )
-    locals_ = [pltpu.make_async_copy(sources[a], mine[a], local_sems.at[a]) for a in range(3)]
-    for copy in locals_:
-        copy.start()
-    for a in range(3):
-        for j in range(1, PLANE):
-            sent.remote(
-                sources[a],
-                mine[a],
-                fan_send.at[a, 0, j],
-                attn_recv.at[a, d],
-                (place.plane_chip(j), f),
-            )
-
-    mats = (gate_ref, up_ref, down_ref)
-
-    three_copies = []
-    for k in range(place.groups):
-        for b in range(2):
-            to_x = (place.x + b) % 2
-            chip = ((place.g + k) % place.groups) * PLANE + 2 * f + to_x
-            slot = 2 * k + b
+        for core in range(2):
+            stage_copy(a, 1, core).start()
+
+        @pl.when(place.y != f)
+        def _():
             for core in range(2):
-                for a in range(3):
-                    src = mats[a].at[
-                        pl.ds(half * core, half), pl.ds(pl.multiple_of(part * to_x, 128), part)
-                    ]
-                    dst = full_three.at[a, pl.ds(pl.multiple_of(d * share + half * core, 16), half)]
-                    copy = pltpu.make_async_remote_copy(
-                        src_ref=src,
-                        dst_ref=dst,
-                        send_sem=three_send.at[a, slot, core],
-                        recv_sem=three_recv.at[a, d],
-                        device_id=(chip, core),
-                        device_id_type=MESH,
-                    )
-                    three_copies.append((slot, copy))
-    for slot, copy in three_copies:
-        if slot == 0:
-            pl.when(place.y != f)(copy.start)
-        else:
-            copy.start()
-
-    def own_parts():
-        band = pl.ds(pl.multiple_of(d * share, 16), share)
-        to = []
-        for a in range(3):
-            src = mats[a].at[:, pl.ds(pl.multiple_of(part * place.x, 128), part)]
-            to.append((src, full_three.at[a, band]))
-        return to
-
-    def own_local():
-        return [
-            pltpu.make_async_copy(src, dst, local_sems.at[3 + a])
-            for a, (src, dst) in enumerate(own_parts())
-        ]
-
-    def own_remote():
-        return [
-            pltpu.make_async_remote_copy(
-                src_ref=src,
-                dst_ref=dst,
-                send_sem=own_sems.at[0, a],
-                recv_sem=own_sems.at[1, a],
-                device_id=(d, other),
-                device_id_type=MESH,
-            )
-            for a, (src, dst) in enumerate(own_parts())
-        ]
-
-    @pl.when(place.y == f)
-    def _():
-        for copy in own_local() + own_remote():
-            copy.start()
+                stage_copy(a, 0, core).start()
+
+        @pl.when(place.y == f)
+        def _():
+            own_copy(a).start()
+            pair_copy(a).start()
 
     for k in range(1, chips):
-        arrived(deal_all.at[(d + k) % chips], deal_recv.at[(d + k) % chips])
+        s = (d + k) % chips
+        arrived(deal_all.at[s], deal_recv.at[s])
+    chip_bits = (2 * rows).bit_length() - 1
     deals = deal_all[:, 0, :]
-    chip_bits = (2 * rows).bit_length() - 1
     wants = lax.shift_right_logical(deals, chip_bits) == d
     offset = deals & (rows - 1)
     earlier = (iota((rows, rows), 0) < iota((rows, rows), 1)).astype(BF16)
@@ -630,260 +770,40 @@
     for j in range(chips):
         hit = wants[j : j + 1, :] & (rank[j : j + 1, :] == iota((per, rows), 0).astype(F32))
         index = jnp.sum(jnp.where(hit, offset[j : j + 1, :], 0), axis=1, keepdims=True)
-        take_ref[j * per : (j + 1) * per, :] = (index == iota((per, rows), 1)).astype(F32).astype(BF16)
-    give[:, :width] = mm(take_ref[...], tokens_ref[...]).astype(BF16)
-    give[:, width:] = mm(take_ref[...], cot_ref[...]).astype(BF16)
+        take_ref[j * per : (j + 1) * per, :] = (
+            (index == iota((per, rows), 1)).astype(F32).astype(BF16)
+        )
 
     def block(k):
         return pl.ds(pl.multiple_of(k * per, per), per)
 
-    for k in range(1, chips):
-        to = (d + k) % chips
-        sent.remote(give.at[block(to)], got.at[block(d)], row_send.at[k], row_recv.at[d], (to, f))
-    got[block(d), :] = give[block(d), :]
-
-    for k in range(1, place.groups):
-        s = place.column_chip(k)
-        piece = attn_slices(s)
-        for a in range(3):
-            arrived(piece[a], attn_recv.at[a, s])
-            for j in range(1, PLANE):
-                sent.remote(
-                    piece[a],
-                    piece[a],
-                    fan_send.at[a, k, j],
-                    attn_recv.at[a, s],
-                    (place.plane_chip(j), f),
-                )
-
-    source_col = lax.shift_right_logical(deal_col_ref[...], chip_bits)
-    source_row = lax.shift_right_logical(deal_ref[0:1, :], chip_bits)
-    same = (source_col == source_row) & (iota((rows, rows), 1) < iota((rows, rows), 0))
-    order = jnp.sum(same.astype(F32), axis=1, keepdims=True).astype(jnp.int32)
-    where_from = source_col * per + order
-    place_ref[...] = (where_from == iota((rows, rows), 1)).astype(F32).astype(BF16)
-    for k in range(1, chips):
-        s = (d + k) % chips
-        arrived(got.at[block(s)], row_recv.at[s])
-    rows_out[...] = mm(place_ref[...], got[:, :width]).astype(BF16)
-    pg_all[place.p] = mm(place_ref[...], got[:, width:]).astype(BF16)
-    for j in range(1, PLANE):
-        sent.remote(
-            pg_all.at[place.p],
-            pg_all.at[place.p],
-            pg_send.at[j],
-            pg_recv.at[place.p],
-            (place.plane_chip(j), f),
-        )
-
-    for k in range(place.groups):
-        for j in range(PLANE):
-            s = ((place.g + k) % place.groups) * PLANE + place.plane_pos(j)
-            if k == 0 and j == 0:
-                continue
-            band = pl.ds(pl.multiple_of(s * share + half * f, 16), half)
-            for a in range(3):
-                piece = full_three.at[a, band]
-                arrived(piece, three_recv.at[a, s])
-                sent.remote(piece, piece, relay_send.at[a, s], relay_recv.at[a, s], (d, other))
-    for k in range(place.groups):
-        for j in range(1, PLANE):
-            s = ((place.g + k) % place.groups) * PLANE + place.plane_pos(j)
-            piece = attn_slices(s)
-            for a in range(3):
-                arrived(piece[a], attn_recv.at[a, s])
-    for copy in locals_:
-        copy.wait()
-    sent.remote(full_kvg.at[f], full_kvg.at[f], kv_sems.at[0], kv_sems.at[1], (d, other))
-    for j in range(1, PLANE):
-        pos = place.plane_pos(j)
-        arrived(pg_all.at[pos], pg_recv.at[pos])
-    for k in range(place.groups):
-        for j in range(PLANE):
-            s = ((place.g + k) % place.groups) * PLANE + place.plane_pos(j)
-            if k == 0 and j == 0:
-                continue
-            band = pl.ds(pl.multiple_of(s * share + half * other, 16), half)
-            for a in range(3):
-                arrived(full_three.at[a, band], relay_recv.at[a, s])
-
-    @pl.when(place.y == f)
-    def _():
-        for copy in own_local():
-            copy.wait()
-        for copy in own_remote():
-            copy.wait_send()
-
-    @pl.when(place.y != f)
-    def _():
-        for copy in own_remote():
-            copy.wait_recv()
-
-    arrived(full_kvg.at[other], kv_sems.at[1])
-    for slot, copy in three_copies:
-        if slot == 0:
-            pl.when(place.y != f)(copy.wait_send)
-        else:
-            copy.wait_send()
-    sent.finish()
-
-
-def gather(chips, deal, tokens, cotangent, wq, wot, kvg, gate, up, down):
-    rows, width = tokens.shape
-    share = wq.shape[0]
-    groups = chips // PLANE
-    part = gate.shape[1] // 2
-    dma = pltpu.SemaphoreType.DMA
-    deal_rows = jnp.broadcast_to(deal[None, :], (8, rows))
-    deal_col = jnp.broadcast_to(deal[:, None], (rows, rows))
-    return pl.pallas_call(
-        functools.partial(gather_kernel, chips),
-        out_shape=(
-            jax.ShapeDtypeStruct((width, wq.shape[1]), BF16),
-            jax.ShapeDtypeStruct((width, wq.shape[1]), BF16),
-            jax.ShapeDtypeStruct((2, chips) + kvg.shape, BF16),
-            jax.ShapeDtypeStruct((3, width, part), BF16),
-            jax.ShapeDtypeStruct((rows, width), BF16),
-            jax.ShapeDtypeStruct((PLANE, rows, width), BF16),
-            jax.ShapeDtypeStruct((rows, rows), BF16),
-            jax.ShapeDtypeStruct((rows, rows), BF16),
-        ),
-        in_specs=[VM] * 4 + [ANY] * 6,
-        out_specs=(ANY, ANY, ANY, ANY, VM, VM, VM, VM),
-        scratch_shapes=[
-            pltpu.VMEM((chips, 8, rows), jnp.int32),
-            pltpu.VMEM((rows, 2 * width), BF16),
-            pltpu.VMEM((rows, 2 * width), BF16),
-            dma((chips,)),
-            dma((chips,)),
-            dma((chips,)),
-            dma((chips,)),
-            dma((3, groups)),
-            dma((3, chips)),
-            dma((3, groups, PLANE)),
-            dma((2,)),
-            dma((3, 2 * groups, 2)),
-            dma((3, chips)),
-            dma((3, chips)),
-            dma((3, chips)),
-            dma((2, 3)),
-            dma((PLANE,)),
-            dma((PLANE,)),
-            dma((6,)),
-        ],
-        compiler_params=pltpu.CompilerParams(
-            collective_id=0, has_side_effects=True, vmem_limit_bytes=VMEM_ASK
-        ),
-        name="gather_weights_and_rows",
-    )(deal_rows, deal_col, tokens, cotangent, wq, wot, kvg, gate, up, down)
-
-
-def rms_scale(values):
-    return lax.rsqrt(jnp.mean(values * values, axis=-1, keepdims=True) + EPSILON)
-
-
-def turned(values, cosine, sine):
-    return values * cosine + pltpu.roll(values, HEAD // 2, 1) * sine
-
-
-def halves_in(first, second):
-    front = iota(first.shape, 1) < HEAD // 2
-    return (
-        jnp.where(front, first, pltpu.roll(second, HEAD // 2, 1)),
-        jnp.where(front, pltpu.roll(first, HEAD // 2, 1), second),
-    )
-
-
-def attention_kernel(
-    chips,
-    reach,
-    first_ref,
-    rows_ref,
-    wq_ref,
-    wot_ref,
-    kvg_ref,
-    cos_ref,
-    sin_ref,
-    n1_ref,
-    qs_ref,
-    kv_ref,
-    probs_ref,
-    mixed_ref,
-    middle_ref,
-    n2_ref,
-    bias_ref,
-    branch_out,
-    branch_in,
-    n1_sems,
-    kv_send,
-    kv_recv,
-    branch_sems,
-):
-    place = Place(chips)
-    d, f, other = place.d, place.f, place.other
-    rows, width = rows_ref.shape
-    micro = rows // MICRO
-    heads = wq_ref.shape[1] // HEAD
-    share = width // chips
-    slots = 2 * reach + 2
-    span = (2 * reach + 1) * micro
-    sent = Sent()
-    greet_all(place)
-
-    row_values = rows_ref[...].astype(F32)
-    gain_one = gain_row(kvg_ref, 0, chips, width, share)
-    n1_ref[f] = (row_values * rms_scale(row_values) * gain_one).astype(BF16)
-    sent.remote(n1_ref.at[f], n1_ref.at[f], n1_sems.at[0], n1_sems.at[1], (d, other))
-
-    kvw = [kvg_ref[i, :, 0:share, :].reshape(width, HEAD) for i in range(2)]
-    raw = [mm(n1_ref[f], kvw[i]) for i in range(2)]
-    key_raw, value_raw = halves_in(raw[0], raw[1])
-    for m in range(MICRO):
-        hm = 2 * f + m
-        band = slice(m * micro, (m + 1) * micro)
-        key = turned(key_raw[band], cos_ref[hm], sin_ref[hm])
-        kv_ref[m, 2 * reach + f, :, 0:HEAD] = key.astype(BF16)
-        kv_ref[m, 2 * reach + f, :, HEAD:] = value_raw[band].astype(BF16)
-    own_kv = kv_ref.at[:, 2 * reach + f]
-
-    def kv_copy(j, core):
-        slot = 2 * reach + f - 2 * j
-        return pltpu.make_async_remote_copy(
-            src_ref=own_kv,
-            dst_ref=kv_ref.at[:, slot],
-            send_sem=kv_send.at[j, core],
-            recv_sem=kv_recv.at[slot],
-            device_id=(d + j, core),
-            device_id_type=MESH,
-        )
-
-    sent.remote(
-        own_kv, own_kv, kv_send.at[0, 0], kv_recv.at[2 * reach + f], (d, other)
-    )
-    for j in range(1, reach + 1):
-
-        @pl.when(d + j < chips)
-        def _():
-            for core in range(2):
-                kv_copy(j, core).start()
-
-        @pl.when(d - j < 0)
-        def _():
-            for core in range(2):
-                kv_ref[:, 2 * reach - 2 * j + core] = jnp.zeros((MICRO, micro, 2 * HEAD), BF16)
-
-    def project(h):
-        raw_q = mm(n1_ref[h], wq_ref[...])
-        for m in range(MICRO):
-            hm = 2 * h + m
-            cosine, sine = cos_ref[hm], sin_ref[hm]
-            for i in range(heads):
-                one = raw_q[m * micro : (m + 1) * micro, i * HEAD : (i + 1) * HEAD]
-                qs_ref[hm, i * micro : (i + 1) * micro, :] = turned(one, cosine, sine).astype(BF16)
-
-    project(f)
-    arrived(n1_ref.at[other], n1_sems.at[1])
-    project(other)
+    def give_rows(i, source_ref):
+        give[i] = mm(take_ref[...], source_ref[...]).astype(BF16)
+        for k in range(1, chips):
+            to = (d + k) % chips
+            sent.remote(
+                give.at[i, block(to)],
+                got.at[i, block(d)],
+                row_send.at[i, k],
+                row_recv.at[i, d],
+                (to, f),
+            )
+        got[i, block(d), :] = give[i, block(d), :]
+
+    def take_rows(i):
+        for k in range(1, chips):
+            s = (d + k) % chips
+            arrived(got.at[i, block(s)], row_recv.at[i, s])
+        return mm(place_ref[...], got[i])
+
+    give_rows(0, tokens_ref)
+    def soon(a, g):
+        if a < 2:
+            fan(a, g)
+
+    def column_pass(k, a):
+        pl.when(place.g >= k)(functools.partial(pass_on, a, place.g - k))
+        pl.when(place.g + k < groups)(functools.partial(pass_on, a, place.g + k))
 
     def make_bias(hm, carry):
         h, m = hm // 2, hm % 2
@@ -900,6 +820,170 @@
         return carry
 
     lax.fori_loop(0, 4, make_bias, 0)
+
+    attn.step(1, (0, 1, 2), soon)
+    pass_on(1, place.g)
+    source_col = lax.shift_right_logical(deal_col_ref[...], chip_bits)
+    source_row = lax.shift_right_logical(deal_ref[0:1, :], chip_bits)
+    same = (source_col == source_row) & (iota((rows, rows), 1) < iota((rows, rows), 0))
+    order = jnp.sum(same.astype(F32), axis=1, keepdims=True).astype(jnp.int32)
+    where_from = source_col * per + order
+    place_ref[...] = (where_from == iota((rows, rows), 1)).astype(F32).astype(BF16)
+    three = Chain(
+        place,
+        lambda a, g: full_three.at[a, pl.ds(g * PLANE, PLANE), f],
+        3,
+        three_up,
+        three_down,
+        three_recv,
+    )
+
+    def relay_copy(a, g):
+        ref = full_three.at[a, pl.ds(g * PLANE, PLANE), f]
+        return pltpu.make_async_remote_copy(
+            src_ref=ref,
+            dst_ref=ref,
+            send_sem=relay_send.at[a, g],
+            recv_sem=relay_recv.at[a, g],
+            device_id=(d, other),
+            device_id_type=MESH,
+        )
+
+    def relay(a, g):
+        relay_copy(a, g).start()
+
+    def three_start(a):
+        for j in range(1, PLANE):
+            pos = place.plane_pos(j)
+            arrived(full_three.at[a, place.g * PLANE + pos, f], stage_recv.at[a, pos])
+
+        @pl.when(place.y == f)
+        def _():
+            own_copy(a).wait()
+
+        @pl.when(place.y != f)
+        def _():
+            arrived(full_three.at[a, d, f], stage_recv.at[a, place.p])
+
+        three.start(a)
+        relay(a, place.g)
+
+    for k in range(2, groups):
+        attn.step(k, (0, 1, 2), soon)
+        column_pass(k - 1, 1)
+        if k == groups - 2:
+            three_start(0)
+            give_rows(1, cot_ref)
+    row_values = take_rows(0)
+    column_pass(groups - 1, 1)
+
+    for g in range(groups):
+        fan(2, g)
+    rows_out[...] = row_values.astype(BF16)
+
+    def attn_wait(a):
+        for g in range(groups):
+            if a == 0:
+                left = range(1, PLANE)
+            else:
+                left = (2 - g % 2, 3)
+            for j in left:
+                s = g * PLANE + place.plane_pos(j)
+                arrived(attn_piece(a, s), fan_recv.at[a, s])
+
+    def spread_copy(i, block_ref, pos, side, to, slot):
+        piece = block_ref.at[pos, pl.ds(side * micro, micro)]
+        return pltpu.make_async_remote_copy(
+            src_ref=piece,
+            dst_ref=piece,
+            send_sem=plane_send.at[i, slot],
+            recv_sem=plane_recv.at[i, pos, side],
+            device_id=(to, f),
+            device_id_type=MESH,
+        )
+
+    by_x, by_y, far = (place.plane_pos(j) for j in range(1, PLANE))
+    to_x, to_y = place.plane_chip(1), place.plane_chip(2)
+
+    def spread(i, block_ref):
+        sends = ((0, to_x), (1, to_y), (1, to_x), (0, to_y))
+        for slot, (side, to) in enumerate(sends):
+            copy = spread_copy(i, block_ref, place.p, side, to, slot)
+            copy.start()
+            sent.copies.append(copy)
+
+    def spread_on(i, block_ref):
+        for slot, pos, side, to in ((4, by_x, 0, to_y), (5, by_y, 1, to_x)):
+            arrived(block_ref.at[pos, pl.ds(side * micro, micro)], plane_recv.at[i, pos, side])
+            copy = spread_copy(i, block_ref, pos, side, to, slot)
+            copy.start()
+            sent.copies.append(copy)
+
+    def spread_wait(i, block_ref):
+        for pos, side in ((by_x, 1), (by_y, 0), (far, 0), (far, 1)):
+            arrived(block_ref.at[pos, pl.ds(side * micro, micro)], plane_recv.at[i, pos, side])
+
+    attn_wait(0)
+    sent.remote(full_kvg.at[f], full_kvg.at[f], kvg_sems.at[0], kvg_sems.at[1], (d, other))
+    arrived(full_kvg.at[other], kvg_sems.at[1])
+
+    gain_one = gain_row(full_kvg, 0, chips, width, share)
+    n1_ref[f] = (row_values * rms_scale(row_values) * gain_one).astype(BF16)
+    sent.remote(n1_ref.at[f], n1_ref.at[f], n1_sems.at[0], n1_sems.at[1], (d, other))
+
+    kvw = [full_kvg[i, :, 0:share, :].reshape(width, HEAD) for i in range(2)]
+    raw = [mm(n1_ref[f], kvw[i]) for i in range(2)]
+    key_raw, value_raw = halves_in(raw[0], raw[1])
+    for m in range(MICRO):
+        hm = 2 * f + m
+        band = slice(m * micro, (m + 1) * micro)
+        key = turned(key_raw[band], cos_ref[hm], sin_ref[hm])
+        kv_ref[m, 2 * reach + f, :, 0:HEAD] = key.astype(BF16)
+        kv_ref[m, 2 * reach + f, :, HEAD:] = value_raw[band].astype(BF16)
+    own_kv = kv_ref.at[:, 2 * reach + f]
+
+    def kv_copy(j, core):
+        slot = 2 * reach + f - 2 * j
+        return pltpu.make_async_remote_copy(
+            src_ref=own_kv,
+            dst_ref=kv_ref.at[:, slot],
+            send_sem=kv_send.at[j, core],
+            recv_sem=kv_recv.at[slot],
+            device_id=(d + j, core),
+            device_id_type=MESH,
+        )
+
+    sent.remote(own_kv, own_kv, kv_send.at[0, 0], kv_recv.at[2 * reach + f], (d, other))
+    for j in range(1, reach + 1):
+
+        @pl.when(d + j < chips)
+        def _():
+            for core in range(2):
+                kv_copy(j, core).start()
+
+        @pl.when(d - j < 0)
+        def _():
+            for core in range(2):
+                kv_ref[:, 2 * reach - 2 * j + core] = jnp.zeros((MICRO, micro, 2 * HEAD), BF16)
+
+    three_start(1)
+    three_start(2)
+
+    def project(h):
+        raw_q = mm(n1_ref[h], full_q[...])
+        for m in range(MICRO):
+            hm = 2 * h + m
+            cosine, sine = cos_ref[hm], sin_ref[hm]
+            for i in range(heads):
+                one = raw_q[m * micro : (m + 1) * micro, i * HEAD : (i + 1) * HEAD]
+                qs_ref[hm, i * micro : (i + 1) * micro, :] = turned(one, cosine, sine).astype(BF16)
+
+    attn_wait(1)
+    project(f)
+    arrived(n1_ref.at[other], n1_sems.at[1])
+    project(other)
+    three.step(1, (0,), relay)
+
     arrived(kv_ref.at[:, 2 * reach + other], kv_recv.at[2 * reach + other])
     for j in range(1, reach + 1):
 
@@ -911,12 +995,14 @@
 
     score_scale = HEAD ** (-0.5)
 
-    def attend(hm, carry):
+    def attend(hm):
         h, m = hm // 2, hm % 2
-        keys = kv_ref[m, pl.ds(h, 2 * reach + 1), :, 0:HEAD].reshape(span, HEAD)
-        values_t = kv_ref[m, pl.ds(h, 2 * reach + 1), :, HEAD:].reshape(span, HEAD).T
-        for pair in range(heads // 2):
-            band = slice(pair * 2 * micro, (pair + 1) * 2 * micro)
+        keys = kv_ref[m, h : h + 2 * reach + 1, :, 0:HEAD].reshape(span, HEAD)
+        values_t = kv_ref[m, h : h + 2 * reach + 1, :, HEAD:].reshape(span, HEAD).T
+
+        def pair_step(pair, carry):
+            start = pl.multiple_of(pair * 2 * micro, 2 * micro)
+            band = pl.ds(start, 2 * micro)
             bias = bias_ref[hm]
             scores = mm_nt(keys, qs_ref[hm, band, :]) * score_scale + jnp.concatenate(
                 [bias, bias], axis=1
@@ -926,25 +1012,71 @@
             probs = (exp_scores * (1.0 / total)).astype(BF16)
             probs_ref[hm, :, band] = probs
             out_t = mm(values_t, probs)
-            for i in range(2):
-                one = out_t[:, i * micro : (i + 1) * micro].T
-                head = pair * 2 + i
-                mixed_ref[hm, :, head * HEAD : (head + 1) * HEAD] = one.astype(BF16)
-        return carry
-
-    lax.fori_loop(0, 4, attend, 0)
+            mixed_ref[hm, :, band] = jnp.concatenate(
+                [out_t[:, i * micro : (i + 1) * micro].T for i in range(2)], axis=1
+            ).astype(BF16)
+            return carry
+
+        lax.fori_loop(0, heads // 2, pair_step, 0)
+
+    attend(0)
+    three.step(1, (1,), relay)
+    pass_all(2)
+    pg_all[place.p] = take_rows(1).astype(BF16)
+    spread(0, pg_all)
+    attend(1)
+    three.step(1, (2,), relay)
+    attend(2)
+    three.step(2, (0,), relay)
+    attend(3)
 
     def branch(h):
-        return mm_nt(mixed_ref[pl.ds(2 * h, 2)].reshape(rows, heads * HEAD), wot_ref[...])
-
+        return mm_nt(mixed_ref[pl.ds(2 * h, 2)].reshape(rows, heads * HEAD), full_ot[...])
+
+    attn_wait(2)
+    spread_on(0, pg_all)
     branch_out[...] = branch(other).astype(BF16)
     sent.remote(branch_out, branch_in, branch_sems.at[0], branch_sems.at[1], (d, other))
     own = branch(f)
     arrived(branch_in, branch_sems.at[1])
-    middle = row_values + own + branch_in[...].astype(F32)
+    middle = rows_out[...].astype(F32) + own + branch_in[...].astype(F32)
     middle_ref[...] = middle
-    gain_two = gain_row(kvg_ref, 1, chips, width, share)
-    n2_ref[...] = (middle * rms_scale(middle) * gain_two).astype(BF16)
+    gain_two = gain_row(full_kvg, 1, chips, width, share)
+    n2_all[place.p] = (middle * rms_scale(middle) * gain_two).astype(BF16)
+    spread(1, n2_all)
+    three.step(2, (1,), relay)
+    spread_on(1, n2_all)
+    three.step(2, (2,), relay)
+    for k in range(3, groups):
+        three.step(k, (0, 1, 2), relay)
+
+    for g in range(groups):
+        for a in range(3):
+            arrived(full_three.at[a, pl.ds(g * PLANE, PLANE), other], relay_recv.at[a, g])
+    spread_wait(0, pg_all)
+    spread_wait(1, n2_all)
+
+    attn.finish()
+    three.finish()
+    for g in range(groups):
+        for a in range(3):
+            relay_copy(a, g).wait_send()
+            for j in range(1, PLANE if a == 0 else PLANE - 1):
+                fan_copy(a, g, j).wait_send()
+            if a > 0:
+                pass_copy(a, g).wait_send()
+    for a in range(3):
+        for core in range(2):
+            stage_copy(a, 1, core).wait_send()
+
+        @pl.when(place.y != f)
+        def _():
+            for core in range(2):
+                stage_copy(a, 0, core).wait_send()
+
+        @pl.when(place.y == f)
+        def _():
+            pair_copy(a).wait_send()
 
     for j in range(1, reach + 1):
 
@@ -956,53 +1088,88 @@
     sent.finish()
 
 
-def attention(chips, reach, first_len, rows_in, wq, wot, kvg, cosine, sine):
-    rows, width = rows_in.shape
+def forward(chips, reach, first_len, deal, cosine, sine, tokens, cotangent, wq, wot, kvg, gate, up, down):
+    rows, width = tokens.shape
+    share = wq.shape[0]
+    groups = chips // PLANE
+    part = gate.shape[1] // 2
     micro = rows // MICRO
     heads = wq.shape[1] // HEAD
     slots = 2 * reach + 2
     span = (2 * reach + 1) * micro
     dma = pltpu.SemaphoreType.DMA
     shape = jax.ShapeDtypeStruct
+    deal_rows = jnp.broadcast_to(deal[None, :], (8, rows))
+    deal_col = jnp.broadcast_to(deal[:, None], (rows, rows))
     return pl.pallas_call(
-        functools.partial(attention_kernel, chips, reach),
+        functools.partial(forward_kernel, chips, reach),
         out_shape=(
+            shape((3, chips, 2, share // 2, part), BF16),
+            shape((width, wq.shape[1]), BF16),
+            shape((width, wq.shape[1]), BF16),
+            shape((2, chips) + kvg.shape, BF16),
+            shape((rows, width), BF16),
+            shape((PLANE, rows, width), BF16),
+            shape((rows, rows), BF16),
+            shape((rows, rows), BF16),
             shape((2, rows, width), BF16),
             shape((4, heads * micro, HEAD), BF16),
             shape((MICRO, slots, micro, 2 * HEAD), BF16),
             shape((4, span, heads * micro), BF16),
             shape((4, micro, heads * HEAD), BF16),
             shape((rows, width), F32),
-            shape((rows, width), BF16),
+            shape((PLANE, rows, width), BF16),
         ),
-        in_specs=[SM] + [VM] * 6,
-        out_specs=(VM,) * 7,
+        in_specs=[SM] + [VM] * 6 + [ANY] * 6,
+        out_specs=(ANY,) + (VM,) * 14,
         scratch_shapes=[
+            pltpu.VMEM((chips, 8, rows), jnp.int32),
+            pltpu.VMEM((2, rows, width), BF16),
+            pltpu.VMEM((2, rows, width), BF16),
             pltpu.VMEM((4, span, micro), F32),
             pltpu.VMEM((rows, width), BF16),
             pltpu.VMEM((rows, width), BF16),
+            dma((chips,)),
+            dma((chips,)),
+            dma((2, chips)),
+            dma((2, chips)),
+            dma((3, groups)),
+            dma((3, groups)),
+            dma((3, groups)),
+            dma((3, groups, PLANE)),
+            dma((3, chips)),
+            dma((2,)),
+            dma((3, 2, 2)),
+            dma((3, PLANE)),
+            dma((3, groups)),
+            dma((3, groups)),
+            dma((3, groups)),
+            dma((3, groups)),
+            dma((3, groups)),
+            dma((2, 6)),
+            dma((2, PLANE, 2)),
             dma((2,)),
             dma((reach + 1, 2)),
             dma((slots,)),
             dma((2,)),
+            dma((3,)),
         ],
         compiler_params=pltpu.CompilerParams(
-            collective_id=1, has_side_effects=True, vmem_limit_bytes=VMEM_ASK
+            collective_id=0, has_side_effects=True, vmem_limit_bytes=VMEM_ASK
         ),
-        name="attention_forward",
-    )(first_len, rows_in, wq, wot, kvg, cosine, sine)
+        name="gather_and_attention",
+    )(first_len, deal_rows, deal_col, cosine, sine, tokens, cotangent, wq, wot, kvg, gate, up, down)
 
 
 def mlp_kernel(
     chips,
-    n2_ref,
+    n2_all,
     middle_ref,
     pg_ref,
     three_ref,
     out_ref,
     two_ref,
     grads_ref,
-    n2_all,
     turned_ref,
     hidden_ref,
     gate_rows_ref,
@@ -1011,8 +1178,6 @@
     two_got,
     out_give,
     out_got,
-    n2_send,
-    n2_recv,
     two_send,
     two_recv,
     out_send,
@@ -1020,16 +1185,8 @@
 ):
     place = Place(chips)
     f, p = place.f, place.p
-    rows, width = n2_ref.shape
-    part = three_ref.shape[2]
+    rows, width = middle_ref.shape
     greet_all(place)
-    sent = Sent()
-    n2_all[p] = n2_ref[...]
-    for j in range(1, PLANE):
-        sent.remote(
-            n2_all.at[p], n2_all.at[p], n2_send.at[j], n2_recv.at[p], (place.plane_chip(j), f)
-        )
-
     def two_copy(j):
         return pltpu.make_async_remote_copy(
             src_ref=two_give.at[j - 1],
@@ -1055,11 +1212,6 @@
 
     def one_block(j, carry):
         pos = place.plane_pos(j)
-
-        @pl.when(j > 0)
-        def _():
-            arrived(n2_all.at[pos], n2_recv.at[pos])
-
         x = n2_all[pos]
         gate = mm(x, three_ref[0])
         upward = mm(x, three_ref[1])
@@ -1138,11 +1290,10 @@
     for j in range(1, PLANE):
         two_copy(j).wait_send()
         out_copy(j).wait_send()
-    sent.finish()
 
 
 def mlp(chips, n2, middle, pg_all, three):
-    rows, width = n2.shape
+    rows, width = middle.shape
     part = three.shape[2]
     dma = pltpu.SemaphoreType.DMA
     shape = jax.ShapeDtypeStruct
@@ -1157,14 +1308,13 @@
         in_specs=[VM] * 4,
         out_specs=(VM,) * 3,
         scratch_shapes=[
-            pltpu.VMEM((PLANE, rows, width), BF16),
             pltpu.VMEM((width, wide), BF16),
             pltpu.VMEM((wide, part), BF16),
             pltpu.VMEM((wide, part), BF16),
             pltpu.VMEM((wide, part), BF16),
         ]
         + [pltpu.VMEM((PLANE - 1, rows, width), BF16)] * 4
-        + [dma((PLANE,))] * 6,
+        + [dma((PLANE,))] * 4,
         compiler_params=pltpu.CompilerParams(
             collective_id=2, has_side_effects=True, vmem_limit_bytes=VMEM_ASK
         ),
@@ -1745,12 +1895,13 @@
     sine = jnp.concatenate([-sine, sine], axis=1).reshape(4, micro, HEAD)
     gain_rows = jnp.pad(norm_gains, ((0, 15), (0, HEAD - share)))
     kvg = jnp.concatenate([jnp.concatenate([w_key, w_value], axis=1), gain_rows], axis=0)
-    wq, wot, kvg_all, three, rows_in, pg_all, take, placing = gather(
-        chips, deal, tokens, cotangent, w_query, w_out.T, kvg, w_gate, w_up, w_down.T
-    )
-    n1, qs, kv, probs, mixed, middle, n2 = attention(
-        chips, reach, first_len, rows_in, wq, wot, kvg_all, cosine, sine
-    )
+    (
+        three, wq, wot, kvg_all, rows_in, pg_all, take, placing, n1, qs, kv, probs, mixed, middle, n2
+    ) = forward(
+        chips, reach, first_len, deal, cosine, sine, tokens, cotangent, w_query, w_out.T, kvg,
+        w_gate, w_up, w_down.T,
+    )
+    three = three.reshape(3, width, three.shape[-1])
     outs, grad_two, three_grads = mlp(chips, n2, middle, pg_all, three)
     pg = lax.dynamic_index_in_dim(pg_all, d % PLANE, 0, keepdims=False)
     grad_rows, gq, got, gkvg = attention_back(

time: 699 us -> 577 us (0.83)
  Pallas kernels: 676 us -> 547 us
    pallas_call x2 -> x1, Pallas kernels: 278 us -> 173 us  [forward(): pl.pallas_call(functools.partial(forward_kernel, chips, reach), out_shape...]
    pallas_call x1, Pallas kernels: 126 us -> 104 us  [mlp(): pl.pallas_call(functools.partial(mlp_kernel, chips), out_shape=(shape((ro...]
where the time goes in v2:
time: 577 us; the launch traced here: 569 us
  Pallas kernels  547 us (95%)
  local copies, waits for them, and re-layouts  17.3 us (3%)
    pallas_call x1, Pallas kernels, scatter(): pl.pallas_call(functools.partial(scatter_kernel, chips), out_shape=(shape...  213 us
    pallas_call x1, Pallas kernels, forward(): pl.pallas_call(functools.partial(forward_kernel, chips, reach), out_shape...  173 us
    pallas_call x1, Pallas kernels, mlp(): pl.pallas_call(functools.partial(mlp_kernel, chips), out_shape=(shape((ro...  104 us
    pallas_call x1, Pallas kernels, attention_back(): pl.pallas_call(functools.partial(attention_back_kernel, chips, reach), ou...  57.2 us

profile of v2, /device:TPU:26, one launch (start us, length us, event | category | flops | bytes accessed | tf_op | source)
XLA Modules:
  0.0 569.5 jit_solution(9561256439665608925)
XLA Ops:
  0.7 0.1 iota_add_fusion
  0.8 0.7 ge.20
  1.4 0.1 ge.21
  1.5 0.1 subtract_convert_fusion
  1.6 1.3 broadcast_in_dim.14.deal_ref
  2.9 0.8 copy.22
  3.7 0.8 copy.23
  4.5 1.4 fusion.2.kvg_ref
  5.9 1.5 broadcast_in_dim.15.deal_col_ref
  7.3 1.0 fusion
  8.3 1.0 pad_maximum_fusion
  9.3 173.2 %gather_and_attention.1 = (bf16[3,16,2,48,1152]{4,3,2,1,0:T(8,128)(2,1)}, bf16[1536,768]{1,0:T(8,128)(2,1)}, bf16[1536,768]{1,0:T(8,128)(2,1)}, bf16[2,16,112,12...) custom-call(s32[2]{0:T(128)} %first_ref.1, ...), custom_call_target="tpu_custom_call" | custom-call | tf_op jit(solution)/shard_map/gather_and_attention/pallas_call | solution.py:1104
  182.5 103.8 %mlp_both_ways.1 = (bf16[256,1536]{1,0:T(8,128)(2,1)}, f32[256,1536]{1,0:T(8,128)}, bf16[3,1536,1152]{2,1,0:T(8,128)(2,1)}) custom-call(bf16[4,256,1536]{2,1,0:T(8,128)(2,1)} %get-tuple-element.38.n2_all, f32[256,1536]{1,0:T(8,128)} %get-tuple-element.39.middle_ref, bf16[4,256,1536]{2,1,0:T(8,128)(2,1)} %get-tuple-element.40.pg_ref, ...), custom_call_target="tpu_custom_call" | custom-call | tf_op jit(solution)/shard_map/mlp_both_ways/pallas_call | solution.py:1301
  286.4 2.1 dynamic-slice_bitcast_fusion.pg_ref
  288.4 57.2 %attention_backward.1 = (bf16[256,1536]{1,0:T(8,128)(2,1)}, bf16[1536,768]{1,0:T(8,128)(2,1)}, bf16[1536,768]{1,0:T(8,128)(2,1)}, bf16[2,16,112,128]{3,2,1,0:T(8,128)(2,1)}) custom-call(bf16[256,1536]{1,0:T(8,128)(2,1)} %get-tuple-element.43.rows_ref, bf16[256,1536]{1,0:T(8,128)(2,1)} %dynamic-slice_bitcast_fusion.pg_ref, ...), custom_call_target="tpu_custom_call" | custom-call | tf_op jit(solution)/shard_map/attention_backward/pallas_call | solution.py:1559
  345.6 213.3 %scatter_grads_and_rows.1 = (f32[3,96,2304]{2,1,0:T(8,128)}, f32[96,768]{1,0:T(8,128)}, f32[96,768]{1,0:T(8,128)}, f32[112,128]{1,0:T(8,128)}, bf16[256,1536]{1,0:T(8,128)(2,1)}, /*index=5*/bf16[256,1536]{1,0:T(8,128)(2,1)}) custom-call(bf16[3,1536,1152]{2,1,0:T(8,128)(2,1)} %get-tuple-element.42.three_ref, bf16[1536,768]{1,0:T(8,128)(2,1)} %get-tuple-element.53.gq_ref, ...), custom_call_target="tpu_custom_call" | custom-call | tf_op jit(solution)/shard_map/scatter_grads_and_rows/pallas_call | solution.py:1824
  558.9 1.2 slice.23
  560.1 0.9 fusion.3
  561.1 0.7 copy.25
  561.8 0.7 copy.24
  562.5 0.0 copy-start.1
  562.5 0.0 copy-start
  562.5 3.4 slice_bitcast_fusion
  565.8 0.0 copy-start.3
  565.8 0.0 copy-start.2
  565.8 0.0 copy-done.1
  565.8 0.9 copy.30
  566.7 0.0 copy-done
  566.7 0.9 copy.31
  567.6 0.0 copy-done.3
  567.6 0.7 copy.32
  568.3 0.0 copy-done.2
  568.3 0.7 copy.33
  (3 shorter events, 0.0 us)
Async XLA Ops:
  562.5 3.4 copy-start.1
  562.5 4.3 copy-start
  565.8 1.8 copy-start.3
  565.8 2.5 copy-start.2
